TPU v7x, 1024 devices: a whole 8x8x8 slice. The times are simulated.
1024 devices in a mesh: users: 64 (over z, x), items: 16 (over y, core).
Axes of the slice: x: 8, y: 8, z: 8, core: 2. Of those that a mesh axis runs over, the one named last changes fastest.
Arguments:
- confidence: bfloat16 [64, 16, 3, 512, 512], P('users', 'items'), may hold values from 1 to 30
- tile_block: int32 [64, 16, 3], P('users', 'items'), may hold values from 0 to 7, as said below
- tile_count: int32 [64, 16], P('users', 'items'), may hold values from 1 to 3, as said below
- item_factors: bfloat16 [65536, 256], P(('items', 'users')), may hold values from -4 to 4
Outputs:
- solution: float32 [32768, 256], P(('users', 'items'))
- residual: float32 [32768, 256], P(('users', 'items'))
Inputs may be any that keep to these rules, and one draw needn't show every extreme that they name: `tile_block`: the live and the dead slots of one cell name different item blocks of its column. `tile_count`: some cell has all 3 slots live.
All inputs are finite; a program needn't handle non-finite values.
Results may differ from a plain program's by a relative error of at most 0.015.
Values may be sent and summed in bfloat16 or wider, within the bound.
No kernel may reach another device: no remote copies, remote signals or barrier semaphores. Data moves between devices by JAX's collectives and lax.ppermute only.
A program may use at most 32 MiB of HBM per device.

v0:
```python
import jax
import jax.numpy as jnp
from jax import lax
from jax.sharding import PartitionSpec as P

STEPS = 2


damping = 0.1


def shards(confidence, tile_block, tile_count, item_factors):
    tile_values = confidence[0, 0]
    block_ids = tile_block[0, 0]
    live_count = tile_count[0, 0]
    slot_total = tile_values.shape[0]
    block_rows = tile_values.shape[1]
    rank_width = item_factors.shape[1]
    column = lax.all_gather(item_factors, "users", axis=0, tiled=True)
    local_gram = lax.dot_general(
        item_factors, item_factors, (((0,), (0,)), ((), ())), preferred_element_type=jnp.float32
    )
    gram = lax.psum(local_gram, ("users", "items"))

    def tile_term(slot, left_rows):
        factors = lax.dynamic_slice_in_dim(column, block_ids[slot] * block_rows, block_rows, 0)
        values = tile_values[slot].astype(jnp.float32)
        if left_rows is None:
            weighted = (1.0 + values).astype(jnp.bfloat16)
        else:
            scores = lax.dot_general(
                left_rows, factors, (((1,), (1,)), ((), ())), preferred_element_type=jnp.float32
            )
            weighted = (values * scores).astype(jnp.bfloat16)
        return jnp.dot(weighted, factors, preferred_element_type=jnp.float32)

    def tile_sum(left_rows):
        empty = jnp.zeros((block_rows, rank_width), jnp.float32)

        def masked(slot, running):
            keep_flag = jnp.where(slot < live_count, 1.0, 0.0).astype(jnp.float32)
            return running + keep_flag * tile_term(slot, left_rows)

        total = lax.fori_loop(0, slot_total, masked, empty)
        return total

    def reduce_rows(partial_sum):
        return lax.psum_scatter(partial_sum, "items", scatter_dimension=0, tiled=True)

    right_side = reduce_rows(tile_sum(None))
    solution = jnp.zeros_like(right_side)
    residual = right_side
    direction = right_side
    norm_now = jnp.sum(residual * residual, axis=1, keepdims=True)
    for step in range(STEPS):
        local = reduce_rows(
            tile_sum(lax.all_gather(direction.astype(jnp.bfloat16), "items", axis=0, tiled=True))
        )
        image = (
            local + jnp.dot(direction, gram, precision=lax.Precision.HIGHEST) + damping * direction
        )
        step_size = norm_now / jnp.sum(direction * image, axis=1, keepdims=True)
        solution = solution + step_size * direction
        residual = residual - step_size * image
        norm_next = jnp.sum(residual * residual, axis=1, keepdims=True)
        direction = residual + norm_next / norm_now * direction
        norm_now = norm_next
    return (solution, residual)


def solution(mesh):
    in_specs = (
        P("users", "items", None, None, None),
        P("users", "items", None),
        P("users", "items"),
        P(("items", "users"), None),
    )
    out_specs = (P(("users", "items"), None), P(("users", "items"), None))
    return jax.shard_map(shards, mesh=mesh, in_specs=in_specs, out_specs=out_specs, check_vma=False)
```

profile of v0, /device:TPU:1, one launch (start us, length us, event | category | flops | bytes accessed | tf_op | source)
XLA Modules:
  0.0 510.2 jit_solution(10829515064962738278)
XLA Ops:
  8.8 103.4 %all-gather.2.cloned.1.call-done = bf16[4096,256]{1,0:T(8,128)(2,1)} async-done(((bf16[64,256]{1,0:T(8,128)(2,1)}), bf16[4096,256]{1,0:T(8,128)(2,1)}) %all-gather.2.cloned.1.call-update) | async-done | bytes 2097168 | tf_op jit(solution)/shard_map/all_gather | solution.py:19
  112.1 12.4 %while.42 = (s32[]{:T(128)}, f32[512,256]{1,0:T(8,128)S(1)}, s32[]{:T(128)}, bf16[3,512,512]{2,1,0:T(8,128)(2,1)}, s32[3]{0:T(128)}, /*index=5*/bf16[4096,256]{1...) while((s32[]{:T(128)}, f32[512,256]{1,0:T(8,128)S(1)}, ...), condition=%wide.region_1.2_spmd.clone, body=%wide.region_0.0_spmd.clone.sunk | while | flops 135397376 | bytes 1835735 | solution.py:44
  112.1 1.2 dynamic_slice.105
  114.7 1.6 fusion.57
  116.3 1.2 dynamic_slice.105
  118.8 1.6 fusion.57
  120.4 1.2 dynamic_slice.105
  123.0 1.6 fusion.57
  126.5 62.0 %reduce-scatter.4.cloned.1.call-done = f32[32,256]{1,0:T(8,128)} async-done(((f32[512,256]{1,0:T(8,128)}), f32[32,256]{1,0:T(8,128)}) %reduce-scatter.4.cloned.1.call-update) | async-done | bytes 32784 | tf_op jit(solution)/shard_map/reduce_scatter | solution.py:48
  189.2 15.7 %all_gather.10 = bf16[512,256]{1,0:T(8,128)(2,1)S(1)} all-gather(bf16[32,256]{1,0:T(8,128)(2,1)S(1)} %convert_element_type.58), channel_id=1, replica_groups=mesh['users'=64,'items'=16] {'items'}, dimensions={0}, use_global_device_ids=true | all-gather | bytes 278528 | tf_op jit(solution)/shard_map/all_gather | solution.py:57
  204.9 13.3 %while.43 = (s32[]{:T(128)}, f32[512,256]{1,0:T(8,128)S(1)}, s32[]{:T(128)}, bf16[3,512,512]{2,1,0:T(8,128)(2,1)}, s32[3]{0:T(128)}, /*index=5*/bf16[4096,256]{1...) while((s32[]{:T(128)}, f32[512,256]{1,0:T(8,128)S(1)}, ...), condition=%wide.region_5.6_spmd.clone, body=%wide.region_4.5_spmd.clone.sunk | while | flops 269615104 | bytes 2362070 | solution.py:44
  204.9 1.2 dynamic_slice.109
  207.4 1.9 fusion.61
  211.9 1.9 fusion.61
  216.3 1.9 fusion.61
  219.1 197.0 %all-reduce.2.cloned.1.call-done = f32[256,256]{1,0:T(8,128)} async-done(((f32[256,256]{1,0:T(8,128)}), f32[256,256]{1,0:T(8,128)}) %all-reduce.2.cloned.1.call-update) | async-done | bytes 262160 | tf_op jit(solution)/shard_map/psum | solution.py:23
  416.1 1.3 multiply_reduce_fusion.2
  417.7 15.7 %all_gather.11 = bf16[512,256]{1,0:T(8,128)(2,1)S(1)} all-gather(bf16[32,256]{1,0:T(8,128)(2,1)S(1)} %get-tuple-element.473), channel_id=1, replica_groups=mesh['users'=64,'items'=16] {'items'}, dimensions={0}, use_global_device_ids=true | all-gather | bytes 278528 | tf_op jit(solution)/shard_map/all_gather | solution.py:57
  433.3 13.4 %while.44 = (s32[]{:T(128)}, f32[512,256]{1,0:T(8,128)S(1)}, s32[]{:T(128)}, bf16[3,512,512]{2,1,0:T(8,128)(2,1)}, s32[3]{0:T(128)}, /*index=5*/bf16[4096,256]{1...) while((s32[]{:T(128)}, f32[512,256]{1,0:T(8,128)S(1)}, ...), condition=%wide.region_11.12_spmd.clone, body=%wide.region_10.11_spmd.clone.sunk | while | flops 269615104 | bytes 2362070 | solution.py:44
  433.3 1.3 dynamic_slice.113
  435.9 1.9 fusion.65
  440.4 1.9 fusion.65
  444.8 1.9 fusion.65
  447.5 53.7 %reduce-scatter.8.cloned.1.call-done = f32[32,256]{1,0:T(8,128)} async-done(((f32[512,256]{1,0:T(8,128)}), f32[32,256]{1,0:T(8,128)}) %reduce-scatter.8.cloned.1.call-update) | async-done | bytes 32784 | tf_op jit(solution)/shard_map/reduce_scatter | solution.py:48
  (39 shorter events, 12.1 us)
Async XLA Ops:
  8.0 104.1 %all-gather.2.cloned.1.call-start = ((), (), s32[]{:S(2)}) async-start(), calls=%async_computation.3 | async-start | bytes 2129920 | tf_op jit(solution)/shard_map/all_gather | solution.py:19
  8.7 179.7 %reduce-scatter.4.cloned.1.call-start = ((), (), s32[]{:S(2)}) async-start(), calls=%async_computation.4 | async-start | bytes 557056 | tf_op jit(solution)/shard_map/reduce_scatter | solution.py:48
  112.1 13.3 %copy-start.5 = (bf16[64,256]{1,0:T(8,128)(2,1)S(1)}, bf16[64,256]{1,0:T(8,128)(2,1)}, u32[]{:S(2)}) copy-start(bf16[64,256]{1,0:T(8,128)(2,1)} %param.13) | copy-start | bytes 98308
  124.6 0.8 copy-start.2
  125.4 290.7 %all-reduce.2.cloned.1.call-start = ((), (), s32[]{:S(2)}) async-start(), calls=%async_computation.6 | async-start | bytes 524288 | tf_op jit(solution)/shard_map/psum | solution.py:23
  126.4 289.7 %reduce-scatter.6.cloned.1.call-start = ((), (), s32[]{:S(2)}) async-start(), calls=%async_computation.5 | async-start | bytes 557056 | tf_op jit(solution)/shard_map/reduce_scatter | solution.py:48
  204.9 211.2 %copy-start.4 = (f32[32,256]{1,0:T(8,128)S(1)}, f32[32,256]{1,0:T(8,128)}, u32[]{:S(2)}) copy-start(f32[32,256]{1,0:T(8,128)} %reduce-scatter.4.cloned.1.call-done) | copy-start | bytes 98308
  218.2 0.8 copy-start.1
  219.0 282.2 %reduce-scatter.8.cloned.1.call-start = ((), (), s32[]{:S(2)}) async-start(), calls=%async_computation.7 | async-start | bytes 557056 | tf_op jit(solution)/shard_map/reduce_scatter | solution.py:48
  433.3 67.9 %copy-start.3 = (f32[256,256]{1,0:T(8,128)S(1)}, f32[256,256]{1,0:T(8,128)}, u32[]{:S(2)}) copy-start(f32[256,256]{1,0:T(8,128)} %all-reduce.2.cloned.1.call-done) | copy-start | bytes 786436
  446.7 0.8 copy-start
Sparse Core Ops, SparseCore 0:
  13.1 99.0 all-gather.1
  125.5 62.8 reduce-scatter.3
  219.1 61.4 reduce-scatter.5
  447.6 53.5 reduce-scatter.7
Sparse Core Ops, SparseCore 1:
  130.6 285.4 all-reduce.1
where the time goes:
time: 511 us; the launch traced here: 510 us
  waiting for transfers between devices  417 us (82%)
  blocking collectives  31.3 us (6%)
  matrix products  19.3 us (4%)
  between operations  15.3 us (3%)
  local copies, waits for them, and re-layouts  13.6 us (3%)
  loops' own time  11.9 us (2%)
    psum x1, waiting for transfers between devices, shards(): gram = lax.psum(local_gram, ('users', 'items'))  197 us
    reduce_scatter x3, waiting for transfers between devices, reduce_rows(): lax.psum_scatter(partial_sum, 'items', scatter_dimension=0, tiled=True)  116 us
    all_gather x1, waiting for transfers between devices, shards(): column = lax.all_gather(item_factors, 'users', axis=0, tiled=True)  103 us
    all_gather x2, blocking collectives, shards(): lax.all_gather(direction.astype(jnp.bfloat16), 'items', axis=0, tiled=True)  31.3 us
    dot_general x9, matrix products, tile_term(): return jnp.dot(weighted, factors, preferred_element_type=jnp.float32)  15.9 us
    another operation x3, loops' own time, tile_sum(): total = lax.fori_loop(0, slot_total, masked, empty)  11.9 us
    dynamic_slice x9, local copies, waits for them, and re-layouts, tile_term(): block_ids[slot] * block_rows  11.2 us
  transfers between devices with their start and end apart: 5, of which 4 were waited for; matrix products, arithmetic and copies ran while one was open for 2% of the time, Pallas kernels for 0%

commit v1 on v0

v1 whole, which is shorter than its diff:
```python
import functools

import jax
import jax.numpy as jnp
from jax import lax
from jax.experimental import pallas as pl
from jax.experimental.pallas import tpu as pltpu
from jax.sharding import Mesh
from jax.sharding import PartitionSpec as P

STEPS = 2
DAMPING = 0.1
ROW_CHUNK = 256
VMEM_BYTES = 24 * 1024 * 1024
LANES = 128
SCALE_ROWS = 16
SCALE_STEPS = 64.0
FULL_SCALE = 32000.0
USERS = ("z", "x")
ITEMS = ("y", "core")


def tile_kernel(with_direction, count_ref, block_ref, tiles_ref, column_ref, *refs):
    if with_direction:
        left_ref, gram_ref, out_ref, total_ref = refs
    else:
        out_ref, total_ref = refs
    slot = pl.program_id(0)
    rows, rank = total_ref.shape

    @pl.when(slot == 0)
    def start():
        if with_direction:
            left = left_ref[...]
            total_ref[...] = jnp.dot(
                left, gram_ref[0], preferred_element_type=jnp.float32
            ) + jnp.dot(left, gram_ref[1], preferred_element_type=jnp.float32)
        else:
            total_ref[...] = jnp.zeros_like(total_ref)

    @pl.when(slot < count_ref[0])
    def add():
        factors = column_ref[:, block_ref[slot]].reshape(rows, rank)
        for at in range(0, rows, ROW_CHUNK):
            chunk = pl.ds(at, ROW_CHUNK)
            values = tiles_ref[0, chunk, :].astype(jnp.float32)
            if with_direction:
                scores = lax.dot_general(
                    left_ref[chunk, :],
                    factors,
                    (((1,), (1,)), ((), ())),
                    preferred_element_type=jnp.float32,
                )
                weighted = (values * scores).astype(jnp.bfloat16)
            else:
                weighted = (1.0 + values).astype(jnp.bfloat16)
            total_ref[chunk, :] += jnp.dot(weighted, factors, preferred_element_type=jnp.float32)

    @pl.when(slot == pl.num_programs(0) - 1)
    def finish():
        encode(total_ref, out_ref)


def encode(total_ref, out_ref):
    owners = out_ref.shape[0]
    share = total_ref.shape[0] // owners
    for owner in range(owners):
        block = total_ref[pl.ds(owner * share, share), :]
        largest = jnp.max(jnp.abs(block), axis=(0, 1), keepdims=True)
        level = jnp.ceil(jnp.log(jnp.maximum(largest, 1e-30)) * SCALE_STEPS)
        whole = jnp.round(block * (FULL_SCALE * jnp.exp(level * (-1.0 / SCALE_STEPS))))
        whole = whole.astype(jnp.int32).astype(jnp.int16)
        for at in range(0, block.shape[1], LANES):
            out_ref[owner, pl.ds(at // LANES * share, share), :] = whole[:, at : at + LANES]
        out_ref[owner, pl.ds(out_ref.shape[1] - SCALE_ROWS, SCALE_ROWS), :] = jnp.broadcast_to(
            level.astype(jnp.int32), (SCALE_ROWS, LANES)
        ).astype(jnp.int16)


def decode(parts, share, rank):
    levels = parts[:, -1:, :1].astype(jnp.float32)
    values = parts[:, : share * rank // LANES].astype(jnp.float32)
    total = jnp.sum(values * (jnp.exp(levels * (1.0 / SCALE_STEPS)) * (1.0 / FULL_SCALE)), axis=0)
    return jnp.concatenate([total[at : at + share] for at in range(0, total.shape[0], share)], axis=1)


def tile_sum(owners, count, blocks, tiles, column, left=None, gram=None):
    slots, rows, items = tiles.shape
    rank = column.shape[-1]
    whole = pl.BlockSpec(memory_space=pltpu.VMEM)
    scalar = pl.BlockSpec(memory_space=pltpu.SMEM)
    extra = () if left is None else (left, gram)
    return pl.pallas_call(
        functools.partial(tile_kernel, left is not None),
        grid=(slots,),
        out_shape=jax.ShapeDtypeStruct(
            (owners, rows // owners * rank // LANES + SCALE_ROWS, LANES), jnp.int16
        ),
        in_specs=[
            scalar,
            scalar,
            pl.BlockSpec((1, rows, items), lambda slot: (slot, 0, 0)),
            whole,
        ]
        + [whole] * len(extra),
        out_specs=whole,
        scratch_shapes=[pltpu.VMEM((rows, rank), jnp.float32)],
        compiler_params=pltpu.CompilerParams(vmem_limit_bytes=VMEM_BYTES),
    )(count, blocks, tiles, column, *extra)


def exchange(parts, axes):
    return lax.all_to_all(parts, axes, 0, 0, tiled=True)


def gather(block, axes):
    size = lax.axis_size(axes)
    return exchange(jnp.broadcast_to(block[None], (size,) + block.shape), axes)


def shards(confidence, tile_block, tile_count, item_factors):
    tiles = confidence[0, 0]
    blocks = tile_block[0, 0]
    count = tile_count[0]
    rows = tiles.shape[1]
    rank = item_factors.shape[1]

    column = gather(gather(item_factors, "z"), "x")
    flat = column.reshape(-1, rank)
    gram = lax.dot_general(
        flat, flat, (((0,), (0,)), ((), ())), preferred_element_type=jnp.float32
    )
    gram_high = gram.astype(jnp.bfloat16)
    gram_low = (gram - gram_high.astype(jnp.float32)).astype(jnp.bfloat16)
    gram = jnp.stack([gram_high, gram_low])

    owners = lax.axis_size(ITEMS)

    def reduce_rows(coded):
        return decode(exchange(coded, ITEMS), rows // owners, rank)

    right_side = reduce_rows(tile_sum(owners, count, blocks, tiles, column))
    solution = jnp.zeros_like(right_side)
    residual = right_side
    direction = right_side
    norm_now = jnp.sum(residual * residual, axis=1, keepdims=True)
    for step in range(STEPS):
        left = gather(direction.astype(jnp.bfloat16), ITEMS).reshape(rows, rank)
        image = (
            reduce_rows(tile_sum(owners, count, blocks, tiles, column, left, gram))
            + DAMPING * direction
        )
        step_size = norm_now / jnp.sum(direction * image, axis=1, keepdims=True)
        solution = solution + step_size * direction
        residual = residual - step_size * image
        norm_next = jnp.sum(residual * residual, axis=1, keepdims=True)
        direction = residual + norm_next / norm_now * direction
        norm_now = norm_next
    return (solution, residual)


def solution(mesh):
    chips = Mesh(mesh.devices.reshape(8, 8, 8, 2), USERS + ITEMS)
    in_specs = (
        P(USERS, ITEMS, None, None, None),
        P(USERS, ITEMS, None),
        P(USERS, ITEMS),
        P(ITEMS + USERS, None),
    )
    out_specs = (P(USERS + ITEMS, None), P(USERS + ITEMS, None))
    return jax.shard_map(shards, mesh=chips, in_specs=in_specs, out_specs=out_specs, check_vma=False)
```

time: 511 us -> 183 us (0.36)
  waiting for transfers between devices: 417 us -> 61.4 us
  blocking collectives: 31.3 us -> 92.9 us
  matrix products: 19.3 us -> 0.76 us
  between operations: 15.3 us -> 1.41 us
  loops' own time: 11.9 us -> 0 us
  starting transfers between devices: 0.2 us -> 10 us
  local copies, waits for them, and re-layouts: 13.6 us -> 5.97 us
  Pallas kernels: 0 us -> 7.55 us
    psum x1 -> x0, waiting for transfers between devices: 197 us -> none  [shards(): gram = lax.psum(local_gram, ('users', 'items'))]
    reduce_scatter x3 -> x0, waiting for transfers between devices: 116 us -> none  [reduce_rows(): lax.psum_scatter(partial_sum, 'items', scatter_dimension=0, tiled=True)]
    all_gather x1 -> x0, waiting for transfers between devices: 103 us -> none  [shards(): column = lax.all_gather(item_factors, 'users', axis=0, tiled=True)]
    all_to_all x0 -> x5, blocking collectives: none -> 92.9 us  [exchange(): return lax.all_to_all(parts, axes, 0, 0, tiled=True)]
    all_to_all x0 -> x2, waiting for transfers between devices: none -> 61.4 us  [exchange(): return lax.all_to_all(parts, axes, 0, 0, tiled=True)]
    all_gather x2 -> x0, blocking collectives: 31.3 us -> none  [shards(): lax.all_gather(direction.astype(jnp.bfloat16), 'items', axis=0, tiled=True)]
    dot_general x12 -> x1, matrix products: 19.3 us -> 0.76 us  [shards(): lax.dot_general(flat, flat, (((0,), (0,)), ((), ())), preferred_element_t...]
    another operation x3 -> x0, loops' own time: 11.9 us -> none  [tile_sum(): total = lax.fori_loop(0, slot_total, masked, empty)]
  transfers between devices with their start and end apart: 5 -> 2, of which waited for: 4 -> 2; matrix products, arithmetic and copies ran while one was open for 2% -> 0% of each run, Pallas kernels for 0% -> 0%
where the time goes in v1:
time: 183 us; the launch traced here: 182 us
  blocking collectives  92.9 us (51%)
  waiting for transfers between devices  61.4 us (34%)
  starting transfers between devices  10 us (5%)
  Pallas kernels  7.55 us (4%)
  local copies, waits for them, and re-layouts  5.97 us (3%)
  other arithmetic  2.35 us (1%)
    all_to_all x5, blocking collectives, exchange(): return lax.all_to_all(parts, axes, 0, 0, tiled=True)  92.9 us
    all_to_all x2, waiting for transfers between devices, exchange(): return lax.all_to_all(parts, axes, 0, 0, tiled=True)  61.4 us
    all_to_all x2, starting transfers between devices, exchange(): return lax.all_to_all(parts, axes, 0, 0, tiled=True)  10 us
    pallas_call x3, Pallas kernels, tile_sum(): pl.pallas_call(functools.partial(tile_kernel, left is not None), grid=(sl...  7.55 us
  transfers between devices with their start and end apart: 2, of which 2 were waited for; matrix products, arithmetic and copies ran while one was open for 0% of the time, Pallas kernels for 0%

profile of v1, /device:TPU:1, one launch (start us, length us, event | category | flops | bytes accessed | tf_op | source)
XLA Modules:
  0.0 182.4 jit_solution(16850554793270466397)
XLA Ops:
  0.6 0.8 broadcast_in_dim.8
  1.4 27.4 %all_to_all.35 = bf16[8,64,256]{2,1,0:T(8,128)(2,1)S(1)} all-to-all(bf16[8,64,256]{2,1,0:T(8,128)(2,1)S(1)} %broadcast_in_dim.8), channel_id=1, replica_groups=mesh['z'=8,'x'=8,'y'=8,'core'=2] {'z'}, dimensions={0} | all-to-all | bytes 524288 | tf_op jit(solution)/shard_map/all_to_all | solution.py:113
  28.8 1.6 broadcast_in_dim.9
  30.4 6.6 %all-to-all-start.1 = ((bf16[8,8,64,256]{3,2,1,0:T(8,128)(2,1)}), bf16[8,8,64,256]{3,2,1,0:T(8,128)(2,1)S(1)}, u32[]{:S(2)}, u32[]{:S(2)}) async-start(bf16[8,8,64,256]{3,2,1,0:T(8,128)(2,1)} %broadcast_in_dim.9), calls=%async_computation.1 | async-start | bytes 4194304 | tf_op jit(solution)/shard_map/all_to_all | solution.py:113
  37.7 51.0 %all-to-all-done.1.column_ref = bf16[8,8,64,256]{3,2,1,0:T(8,128)(2,1)S(1)} async-done(((bf16[8,8,64,256]{3,2,1,0:T(8,128)(2,1)}), bf16[8,8,64,256]{3,2,1,0:T(8,128)(2,1)S(1)}, u32[]{:S(2)}, u32[]{:S(2)}) %all-to-all-start.1) | async-done | bytes 2097184 | tf_op jit(solution)/shard_map/all_to_all | solution.py:113
  88.7 1.4 copy-done
  90.1 1.8 shard_map.59
  91.9 20.6 %all_to_all.36 = s16[16,80,128]{2,1,0:T(8,128)(2,1)S(1)} all-to-all(s16[16,80,128]{2,1,0:T(8,128)(2,1)S(1)} %shard_map.59), channel_id=1, replica_groups=mesh['z'=8,'x'=8,'y'=8,'core'=2] {'y','core'}, dimensions={0} | all-to-all | bytes 655360 | tf_op jit(solution)/shard_map/all_to_all | solution.py:113
  112.5 0.2 fusion.10
  112.9 0.7 broadcast_in_dim.10
  113.6 3.4 %all-to-all-start.3 = ((bf16[16,32,256]{2,1,0:T(8,128)(2,1)}), bf16[16,32,256]{2,1,0:T(8,128)(2,1)S(1)}, u32[]{:S(2)}, u32[]{:S(2)}) async-start(bf16[16,32,256]{2,1,0:T(8,128)(2,1)} %broadcast_in_dim.10), calls=%async_computation.3 | async-start | bytes 524288 | tf_op jit(solution)/shard_map/all_to_all | solution.py:113
  117.0 0.8 convert_bitcast_fusion
  117.8 10.4 %all-to-all-done.3 = bf16[16,32,256]{2,1,0:T(8,128)(2,1)S(1)} async-done(((bf16[16,32,256]{2,1,0:T(8,128)(2,1)}), bf16[16,32,256]{2,1,0:T(8,128)(2,1)S(1)}, u32[]{:S(2)}, u32[]{:S(2)}) %all-to-all-start.3) | async-done | bytes 262176 | tf_op jit(solution)/shard_map/all_to_all | solution.py:113
  128.2 1.4 copy-done.1
  129.6 2.9 %shard_map.60 = s16[16,80,128]{2,1,0:T(8,128)(2,1)S(1)} custom-call(s32[1]{0:T(128)} %bitcast.18.count_ref, s32[3]{0:T(128)S(1)} %bitcast.26, bf16[3,512,512]{2,1,0:T(8,128)(2,1)S(1)} %bitcast.21, bf16[8,8,64,256]{3,2,1,0:T(8,128)(2,1)S(1)} %all-to-all-done.1.column_ref, bf16[512,256]{1,0:T(8,128)(2,1)S(1)} %bitcast.23, ...), custom_call_target="tpu_custom_call" | custom-call | tf_op jit(solution)/shard_map/pallas_call | solution.py:93
  132.5 15.2 %all_to_all.37 = s16[16,80,128]{2,1,0:T(8,128)(2,1)S(1)} all-to-all(s16[16,80,128]{2,1,0:T(8,128)(2,1)S(1)} %shard_map.60), channel_id=1, replica_groups=mesh['z'=8,'x'=8,'y'=8,'core'=2] {'y','core'}, dimensions={0} | all-to-all | bytes 655360 | tf_op jit(solution)/shard_map/all_to_all | solution.py:113
  147.7 0.2 fusion.11
  148.2 0.2 multiply_reduce_fusion.4
  148.5 14.5 %all_to_all.38 = bf16[16,32,256]{2,1,0:T(8,128)(2,1)S(1)} all-to-all(bf16[16,32,256]{2,1,0:T(8,128)(2,1)S(1)} %broadcast_in_dim.11), channel_id=1, replica_groups=mesh['z'=8,'x'=8,'y'=8,'core'=2] {'y','core'}, dimensions={0} | all-to-all | bytes 524288 | tf_op jit(solution)/shard_map/all_to_all | solution.py:113
  163.0 2.9 %shard_map.61 = s16[16,80,128]{2,1,0:T(8,128)(2,1)S(1)} custom-call(s32[1]{0:T(128)} %bitcast.19.count_ref, s32[3]{0:T(128)S(1)} %bitcast.27, bf16[3,512,512]{2,1,0:T(8,128)(2,1)S(1)} %bitcast.22, bf16[8,8,64,256]{3,2,1,0:T(8,128)(2,1)S(1)} %all-to-all-done.1.column_ref, bf16[512,256]{1,0:T(8,128)(2,1)S(1)} %bitcast.24, ...), custom_call_target="tpu_custom_call" | custom-call | tf_op jit(solution)/shard_map/pallas_call | solution.py:93
  165.8 15.2 %all_to_all.39 = s16[16,80,128]{2,1,0:T(8,128)(2,1)S(1)} all-to-all(s16[16,80,128]{2,1,0:T(8,128)(2,1)S(1)} %shard_map.61), channel_id=1, replica_groups=mesh['z'=8,'x'=8,'y'=8,'core'=2] {'y','core'}, dimensions={0} | all-to-all | bytes 655360 | tf_op jit(solution)/shard_map/all_to_all | solution.py:113
  181.1 0.2 fusion.12
  181.4 0.2 multiply_reduce_fusion.3
  181.6 0.7 multiply_subtract_fusion
  (18 shorter events, 0.7 us)
Async XLA Ops:
  30.4 58.3 %copy-start.2 = (s32[1,1,3]{2,1,0:T(1,128)S(1)}, s32[1,1,3]{2,1,0:T(1,128)}, u32[]{:S(2)}) copy-start(s32[1,1,3]{2,1,0:T(1,128)} %param.5) | copy-start | bytes 40
  30.4 58.3 %all-to-all-start.1 = ((bf16[8,8,64,256]{3,2,1,0:T(8,128)(2,1)}), bf16[8,8,64,256]{3,2,1,0:T(8,128)(2,1)S(1)}, u32[]{:S(2)}, u32[]{:S(2)}) async-start(bf16[8,8,64,256]{3,2,1,0:T(8,128)(2,1)} %broadcast_in_dim.9), calls=%async_computation.1 | async-start | bytes 4194304 | tf_op jit(solution)/shard_map/all_to_all | solution.py:113
  88.7 1.4 copy-start
  113.6 14.6 %all-to-all-start.3 = ((bf16[16,32,256]{2,1,0:T(8,128)(2,1)}), bf16[16,32,256]{2,1,0:T(8,128)(2,1)S(1)}, u32[]{:S(2)}, u32[]{:S(2)}) async-start(bf16[16,32,256]{2,1,0:T(8,128)(2,1)} %broadcast_in_dim.10), calls=%async_computation.3 | async-start | bytes 524288 | tf_op jit(solution)/shard_map/all_to_all | solution.py:113
  128.2 1.4 copy-start.1

commit v2 on v1

v2 whole, which is shorter than its diff:
```python
import functools

import jax
import jax.numpy as jnp
from jax import lax
from jax.experimental import pallas as pl
from jax.experimental.pallas import tpu as pltpu
from jax.sharding import Mesh
from jax.sharding import PartitionSpec as P

STEPS = 2
DAMPING = 0.1
ROW_CHUNK = 256
VMEM_BYTES = 24 * 1024 * 1024
LANES = 128
SCALE_ROWS = 8
SCALE_STEPS = 64.0
FULL_SCALE = 32000.0
USERS = ("z", "x")
ITEMS = ("y", "core")
WHOLE = pl.BlockSpec(memory_space=pltpu.VMEM)
SCALARS = pl.BlockSpec(memory_space=pltpu.SMEM)
FAR = pl.BlockSpec(memory_space=pltpu.HBM)


def spread_kernel(first_ref, factors_ref, out_ref):
    piece = factors_ref.shape[0]
    share = out_ref.shape[1] - piece
    gram = jnp.sum(first_ref[:, pl.ds(0, share), :].astype(jnp.float32), axis=0)
    gram = gram.astype(jnp.bfloat16)
    for peer in range(out_ref.shape[0]):
        out_ref[peer, pl.ds(0, piece), :] = factors_ref[...]
        out_ref[peer, pl.ds(piece, share), :] = gram


def spread(first, factors, peers, share):
    piece, rank = factors.shape
    return pl.pallas_call(
        spread_kernel,
        out_shape=jax.ShapeDtypeStruct((peers, piece + share, rank), factors.dtype),
        in_specs=[WHOLE, WHOLE],
        out_specs=WHOLE,
        compiler_params=pltpu.CompilerParams(vmem_limit_bytes=VMEM_BYTES),
    )(first, factors)


def pick_kernel(wanted_ref, pieces_ref, out_ref):
    peers, height, rank = out_ref.shape
    share = rank // peers
    piece = pieces_ref.shape[1] - share
    slots = (height - share) // piece
    gram = jnp.sum(pieces_ref[:, pl.ds(piece, share), :].astype(jnp.float32), axis=0)
    gram = gram.astype(jnp.bfloat16)
    for peer in range(peers):
        for slot in range(slots):
            out_ref[peer, pl.ds(slot * piece, piece), :] = pieces_ref[
                wanted_ref[peer, slot], pl.ds(0, piece), :
            ]
        out_ref[peer, pl.ds(slots * piece, share), :] = gram


def pick(wanted, pieces, slots):
    peers = wanted.shape[0]
    _, height, rank = pieces.shape
    share = rank // peers
    return pl.pallas_call(
        pick_kernel,
        out_shape=jax.ShapeDtypeStruct(
            (peers, slots * (height - share) + share, rank), pieces.dtype
        ),
        in_specs=[SCALARS, WHOLE],
        out_specs=WHOLE,
        compiler_params=pltpu.CompilerParams(vmem_limit_bytes=VMEM_BYTES),
    )(wanted, pieces)


def tile_kernel(with_direction, count_ref, tiles_ref, factors_ref, *refs):
    if with_direction:
        left_ref, out_ref, total_ref, held_ref, arrived = refs
    else:
        out_ref, total_ref, held_ref, arrived = refs
    slots = held_ref.shape[0]
    rows, rank = total_ref.shape
    piece = rows // factors_ref.shape[0]
    step = min(ROW_CHUNK, rows)

    def fetch(slot):
        return pltpu.make_async_copy(tiles_ref.at[slot], held_ref.at[slot], arrived.at[slot])

    for slot in range(slots):

        @pl.when(slot < count_ref[0])
        def ask():
            fetch(slot).start()

    if with_direction:
        share = factors_ref.shape[1] - slots * piece
        gram = factors_ref[:, pl.ds(slots * piece, share), :].reshape(rank, rank)
        total_ref[...] = jnp.dot(left_ref[...], gram, preferred_element_type=jnp.float32)
    else:
        total_ref[...] = jnp.zeros_like(total_ref)

    for slot in range(slots):

        @pl.when(slot < count_ref[0])
        def add():
            factors = factors_ref[:, pl.ds(slot * piece, piece), :].reshape(rows, rank)
            fetch(slot).wait()
            for at in range(0, rows, step):
                chunk = pl.ds(at, step)
                values = held_ref[slot, chunk, :].astype(jnp.float32)
                if with_direction:
                    scores = lax.dot_general(
                        left_ref[chunk, :],
                        factors,
                        (((1,), (1,)), ((), ())),
                        preferred_element_type=jnp.float32,
                    )
                    weighted = (values * scores).astype(jnp.bfloat16)
                else:
                    weighted = (1.0 + values).astype(jnp.bfloat16)
                total_ref[chunk, :] += jnp.dot(
                    weighted, factors, preferred_element_type=jnp.float32
                )

    encode(total_ref, out_ref)


def encode(total_ref, out_ref):
    owners = out_ref.shape[0]
    share = total_ref.shape[0] // owners
    for owner in range(owners):
        block = total_ref[pl.ds(owner * share, share), :]
        largest = jnp.max(jnp.abs(block), axis=(0, 1), keepdims=True)
        level = jnp.ceil(jnp.log(jnp.maximum(largest, 1e-30)) * SCALE_STEPS)
        whole = jnp.round(block * (FULL_SCALE * jnp.exp(level * (-1.0 / SCALE_STEPS))))
        whole = whole.astype(jnp.int32).astype(jnp.int16)
        for at in range(0, block.shape[1], LANES):
            out_ref[owner, pl.ds(at // LANES * share, share), :] = whole[:, at : at + LANES]
        out_ref[owner, pl.ds(out_ref.shape[1] - SCALE_ROWS, SCALE_ROWS), :] = jnp.broadcast_to(
            level.astype(jnp.int32), (SCALE_ROWS, LANES)
        ).astype(jnp.int16)


def decode(parts, share, rank):
    levels = parts[:, -1:, :1].astype(jnp.float32)
    values = parts[:, : share * rank // LANES].astype(jnp.float32)
    total = jnp.sum(values * (jnp.exp(levels * (1.0 / SCALE_STEPS)) * (1.0 / FULL_SCALE)), axis=0)
    return jnp.concatenate([total[at : at + share] for at in range(0, total.shape[0], share)], axis=1)


def tile_sum(owners, count, tiles, factors, left=None):
    slots, rows, items = tiles.shape
    rank = factors.shape[-1]
    extra = () if left is None else (left,)
    return pl.pallas_call(
        functools.partial(tile_kernel, left is not None),
        out_shape=jax.ShapeDtypeStruct(
            (owners, rows // owners * rank // LANES + SCALE_ROWS, LANES), jnp.int16
        ),
        in_specs=[SCALARS, FAR, WHOLE] + [WHOLE] * len(extra),
        out_specs=WHOLE,
        scratch_shapes=[
            pltpu.VMEM((rows, rank), jnp.float32),
            pltpu.VMEM((slots, rows, items), jnp.bfloat16),
            pltpu.SemaphoreType.DMA((slots,)),
        ],
        compiler_params=pltpu.CompilerParams(vmem_limit_bytes=VMEM_BYTES),
    )(count, tiles, factors, *extra)


def exchange(parts, axes):
    return lax.all_to_all(parts, axes, 0, 0, tiled=True)


def gather(block, axes):
    size = lax.axis_size(axes)
    return exchange(jnp.broadcast_to(block[None], (size,) + block.shape), axes)


def shards(confidence, tile_block, tile_count, item_factors):
    tiles = confidence[0, 0]
    blocks = tile_block[0, 0]
    count = tile_count[0]
    slots, rows, _ = tiles.shape
    rank = item_factors.shape[1]
    owners = lax.axis_size(ITEMS)

    peers = lax.axis_size("x")
    share = rank // peers
    local = lax.dot_general(
        item_factors, item_factors, (((0,), (0,)), ((), ())), preferred_element_type=jnp.float32
    ).astype(jnp.bfloat16)
    named = jnp.pad(blocks.astype(jnp.bfloat16), (0, rank - slots))
    first = jnp.concatenate(
        [local.reshape(peers, share, rank), jnp.broadcast_to(named, (peers, 8, rank))], axis=1
    )
    first = exchange(first, "x")
    wanted = first[:, share, :LANES].astype(jnp.int32)
    pieces = exchange(spread(first, item_factors, lax.axis_size("z"), share), "z")
    factors = exchange(pick(wanted, pieces, slots), "x")

    def reduce_rows(coded):
        return decode(exchange(coded, ITEMS), rows // owners, rank)

    right_side = reduce_rows(tile_sum(owners, count, tiles, factors))
    solution = jnp.zeros_like(right_side)
    residual = right_side
    direction = right_side
    norm_now = jnp.sum(residual * residual, axis=1, keepdims=True)
    for step in range(STEPS):
        left = gather(direction.astype(jnp.bfloat16), ITEMS).reshape(rows, rank)
        image = (
            reduce_rows(tile_sum(owners, count, tiles, factors, left))
            + DAMPING * direction
        )
        step_size = norm_now / jnp.sum(direction * image, axis=1, keepdims=True)
        solution = solution + step_size * direction
        residual = residual - step_size * image
        norm_next = jnp.sum(residual * residual, axis=1, keepdims=True)
        direction = residual + norm_next / norm_now * direction
        norm_now = norm_next
    return (solution, residual)


def solution(mesh):
    chips = Mesh(mesh.devices.reshape(8, 8, 8, 2), USERS + ITEMS)
    in_specs = (
        P(USERS, ITEMS, None, None, None),
        P(USERS, ITEMS, None),
        P(USERS, ITEMS),
        P(ITEMS + USERS, None),
    )
    out_specs = (P(USERS + ITEMS, None), P(USERS + ITEMS, None))
    return jax.shard_map(shards, mesh=chips, in_specs=in_specs, out_specs=out_specs, check_vma=False)
```

time: 183 us -> 167 us (0.913)
  waiting for transfers between devices: 61.4 us -> 33.5 us
  starting transfers between devices: 10 us -> 20.1 us
  blocking collectives: 92.9 us -> 99.8 us
  local copies, waits for them, and re-layouts: 5.97 us -> 0.85 us
    all_to_all x2, waiting for transfers between devices: 61.4 us -> 33.5 us  [exchange(): return lax.all_to_all(parts, axes, 0, 0, tiled=True)]
    all_to_all x2, starting transfers between devices: 10 us -> 20.1 us  [exchange(): return lax.all_to_all(parts, axes, 0, 0, tiled=True)]
    all_to_all x5 -> x6, blocking collectives: 92.9 us -> 99.8 us  [exchange(): return lax.all_to_all(parts, axes, 0, 0, tiled=True)]
    broadcast_in_dim x4 -> x2, local copies, waits for them, and re-layouts: 3.13 us -> 0.05 us  [gather(): return exchange(jnp.broadcast_to(block[None], (size,) + block.shape), axes)]
    unnamed x6 -> x4, local copies, waits for them, and re-layouts: 2.82 us -> 0.76 us
    pallas_call x3 -> x5, Pallas kernels: 7.55 us -> 6.83 us  [the longest x3 4.47 us: tile_sum(): pl.pallas_call(functools.partial(tile_kernel, left is not None), out_shap...]
where the time goes in v2:
time: 167 us
  blocking collectives  99.8 us (60%)
  waiting for transfers between devices  33.5 us (20%)
  starting transfers between devices  20.1 us (12%)
  Pallas kernels  6.83 us (4%)
  other arithmetic  3 us (2%)
    all_to_all x6, blocking collectives, exchange(): return lax.all_to_all(parts, axes, 0, 0, tiled=True)  99.8 us
    all_to_all x2, waiting for transfers between devices, exchange(): return lax.all_to_all(parts, axes, 0, 0, tiled=True)  33.5 us
    all_to_all x2, starting transfers between devices, exchange(): return lax.all_to_all(parts, axes, 0, 0, tiled=True)  20.1 us
    pallas_call x3, Pallas kernels, tile_sum(): pl.pallas_call(functools.partial(tile_kernel, left is not None), out_shap...  4.47 us
  transfers between devices with their start and end apart: 2, of which 2 were waited for; matrix products, arithmetic and copies ran while one was open for 0% of the time, Pallas kernels for 0%

profile of v2, /device:TPU:1, one launch (start us, length us, event | category | flops | bytes accessed | tf_op | source)
XLA Modules:
  0.0 166.6 jit_solution(14673780865901295257)
XLA Ops:
  0.6 1.0 convolution_convert_fusion
  1.7 0.7 convert_bitcast_fusion
  2.4 15.4 %all_to_all.40.first_ref = bf16[8,40,256]{2,1,0:T(8,128)(2,1)S(1)} all-to-all(bf16[8,40,256]{2,1,0:T(8,128)(2,1)S(1)} %pad_maximum_fusion), channel_id=1, replica_groups=mesh['z'=8,'x'=8,'y'=8,'core'=2] {'x'}, dimensions={0} | all-to-all | bytes 327680 | tf_op jit(solution)/shard_map/all_to_all | solution.py:173
  17.8 0.8 copy-done.1
  18.5 0.8 shard_map.59
  19.3 16.3 %all-to-all-start.1 = ((bf16[8,96,256]{2,1,0:T(8,128)(2,1)}), bf16[8,96,256]{2,1,0:T(8,128)(2,1)S(1)}, u32[]{:S(2)}, u32[]{:S(2)}) async-start(bf16[8,96,256]{2,1,0:T(8,128)(2,1)} %shard_map.59), calls=%async_computation.1 | async-start | bytes 786432 | tf_op jit(solution)/shard_map/all_to_all | solution.py:173
  35.6 11.3 %all-to-all-done.1.pieces_ref = bf16[8,96,256]{2,1,0:T(8,128)(2,1)S(1)} async-done(((bf16[8,96,256]{2,1,0:T(8,128)(2,1)}), bf16[8,96,256]{2,1,0:T(8,128)(2,1)S(1)}, u32[]{:S(2)}, u32[]{:S(2)}) %all-to-all-start.1) | async-done | bytes 393248 | tf_op jit(solution)/shard_map/all_to_all | solution.py:173
  47.0 1.6 shard_map.60
  48.6 3.9 %all-to-all-start.2 = ((bf16[8,224,256]{2,1,0:T(8,128)(2,1)}), bf16[8,224,256]{2,1,0:T(8,128)(2,1)S(1)}, u32[]{:S(2)}, u32[]{:S(2)}) async-start(bf16[8,224,256]{2,1,0:T(8,128)(2,1)} %shard_map.60), calls=%async_computation.2 | async-start | bytes 1835008 | tf_op jit(solution)/shard_map/all_to_all | solution.py:173
  53.1 22.2 %all-to-all-done.2.factors_ref = bf16[8,224,256]{2,1,0:T(8,128)(2,1)S(1)} async-done(((bf16[8,224,256]{2,1,0:T(8,128)(2,1)}), bf16[8,224,256]{2,1,0:T(8,128)(2,1)S(1)}, u32[]{:S(2)}, u32[]{:S(2)}) %all-to-all-start.2) | async-done | bytes 917536 | tf_op jit(solution)/shard_map/all_to_all | solution.py:173
  75.2 1.0 shard_map.61
  76.3 24.2 %all_to_all.41 = s16[16,72,128]{2,1,0:T(8,128)(2,1)S(1)} all-to-all(s16[16,72,128]{2,1,0:T(8,128)(2,1)S(1)} %shard_map.61), channel_id=1, replica_groups=mesh['z'=8,'x'=8,'y'=8,'core'=2] {'y','core'}, dimensions={0} | all-to-all | bytes 589824 | tf_op jit(solution)/shard_map/all_to_all | solution.py:173
  100.4 0.2 fusion.9
  100.8 14.4 %all_to_all.42 = bf16[16,32,256]{2,1,0:T(8,128)(2,1)S(1)} all-to-all(bf16[16,32,256]{2,1,0:T(8,128)(2,1)S(1)} %broadcast_in_dim.7), channel_id=1, replica_groups=mesh['z'=8,'x'=8,'y'=8,'core'=2] {'y','core'}, dimensions={0} | all-to-all | bytes 524288 | tf_op jit(solution)/shard_map/all_to_all | solution.py:173
  115.3 1.7 %shard_map.62 = s16[16,72,128]{2,1,0:T(8,128)(2,1)S(1)} custom-call(s32[1]{0:T(128)} %bitcast.15.count_ref, bf16[3,512,512]{2,1,0:T(8,128)(2,1)S(1)} %bitcast.18, bf16[8,224,256]{2,1,0:T(8,128)(2,1)S(1)} %all-to-all-done.2.factors_ref, bf16[512,256]{1,0:T(8,128)(2,1)S(1)} %bitcast.21), custom_call_target="tpu_custom_call" | custom-call | tf_op jit(solution)/shard_map/pallas_call | solution.py:156
  117.0 15.7 %all_to_all.43 = s16[16,72,128]{2,1,0:T(8,128)(2,1)S(1)} all-to-all(s16[16,72,128]{2,1,0:T(8,128)(2,1)S(1)} %shard_map.62), channel_id=1, replica_groups=mesh['z'=8,'x'=8,'y'=8,'core'=2] {'y','core'}, dimensions={0} | all-to-all | bytes 589824 | tf_op jit(solution)/shard_map/all_to_all | solution.py:173
  132.7 0.2 fusion.10
  133.2 0.2 multiply_reduce_fusion.4
  133.5 14.4 %all_to_all.44 = bf16[16,32,256]{2,1,0:T(8,128)(2,1)S(1)} all-to-all(bf16[16,32,256]{2,1,0:T(8,128)(2,1)S(1)} %broadcast_in_dim.8), channel_id=1, replica_groups=mesh['z'=8,'x'=8,'y'=8,'core'=2] {'y','core'}, dimensions={0} | all-to-all | bytes 524288 | tf_op jit(solution)/shard_map/all_to_all | solution.py:173
  147.9 1.7 %shard_map.63 = s16[16,72,128]{2,1,0:T(8,128)(2,1)S(1)} custom-call(s32[1]{0:T(128)} %bitcast.16.count_ref, bf16[3,512,512]{2,1,0:T(8,128)(2,1)S(1)} %bitcast.19, bf16[8,224,256]{2,1,0:T(8,128)(2,1)S(1)} %all-to-all-done.2.factors_ref, bf16[512,256]{1,0:T(8,128)(2,1)S(1)} %bitcast.20), custom_call_target="tpu_custom_call" | custom-call | tf_op jit(solution)/shard_map/pallas_call | solution.py:156
  149.6 15.7 %all_to_all.45 = s16[16,72,128]{2,1,0:T(8,128)(2,1)S(1)} all-to-all(s16[16,72,128]{2,1,0:T(8,128)(2,1)S(1)} %shard_map.63), channel_id=1, replica_groups=mesh['z'=8,'x'=8,'y'=8,'core'=2] {'y','core'}, dimensions={0} | all-to-all | bytes 589824 | tf_op jit(solution)/shard_map/all_to_all | solution.py:173
  165.3 0.2 fusion.11
  165.7 0.2 multiply_reduce_fusion.3
  165.9 0.7 multiply_subtract_fusion
  (22 shorter events, 0.7 us)
Async XLA Ops:
  17.8 0.8 copy-start.1
  19.3 27.7 %all-to-all-start.1 = ((bf16[8,96,256]{2,1,0:T(8,128)(2,1)}), bf16[8,96,256]{2,1,0:T(8,128)(2,1)S(1)}, u32[]{:S(2)}, u32[]{:S(2)}) async-start(bf16[8,96,256]{2,1,0:T(8,128)(2,1)} %shard_map.59), calls=%async_computation.1 | async-start | bytes 786432 | tf_op jit(solution)/shard_map/all_to_all | solution.py:173
  35.6 39.6 %copy-start = (bf16[1,1,3,512,512]{4,3,2,1,0:T(8,128)(2,1)S(1)}, bf16[1,1,3,512,512]{4,3,2,1,0:T(8,128)(2,1)}, u32[]{:S(2)}) copy-start(bf16[1,1,3,512,512]{4,3,2,1,0:T(8,128)(2,1)} %param.4) | copy-start | bytes 4718596
  48.6 26.7 %all-to-all-start.2 = ((bf16[8,224,256]{2,1,0:T(8,128)(2,1)}), bf16[8,224,256]{2,1,0:T(8,128)(2,1)S(1)}, u32[]{:S(2)}, u32[]{:S(2)}) async-start(bf16[8,224,256]{2,1,0:T(8,128)(2,1)} %shard_map.60), calls=%async_computation.2 | async-start | bytes 1835008 | tf_op jit(solution)/shard_map/all_to_all | solution.py:173

commit v3 on v2

v3 whole, which is shorter than its diff:
```python
import functools

import jax
import jax.numpy as jnp
from jax import lax
from jax.experimental import pallas as pl
from jax.experimental.pallas import tpu as pltpu
from jax.sharding import Mesh
from jax.sharding import PartitionSpec as P

STEPS = 2
DAMPING = 0.1
ROW_CHUNK = 256
VMEM_BYTES = 24 * 1024 * 1024
LANES = 128
SCALE_ROWS = 8
NAME_ROWS = 8
SCALE_STEPS = 64.0
FULL_SCALE = 32000.0
USERS = ("z", "x")
ITEMS = ("y", "core")
WHOLE = pl.BlockSpec(memory_space=pltpu.VMEM)
SCALARS = pl.BlockSpec(memory_space=pltpu.SMEM)
FAR = pl.BlockSpec(memory_space=pltpu.HBM)


def first_kernel(blocks_ref, pieces_ref, out_ref):
    peers, height, rank = out_ref.shape
    share = rank // peers
    slots = blocks_ref.shape[2]
    flat = pieces_ref[...].reshape(-1, rank)
    gram = lax.dot_general(
        flat, flat, (((0,), (0,)), ((), ())), preferred_element_type=jnp.float32
    ).astype(jnp.bfloat16)
    lane = lax.broadcasted_iota(jnp.int32, (height - share, rank), 1)
    named = jnp.zeros((height - share, rank), jnp.float32)
    for slot in range(slots):
        named = jnp.where(lane == slot, blocks_ref[0, 0, slot].astype(jnp.float32), named)
    for peer in range(peers):
        out_ref[peer, pl.ds(0, share), :] = gram[peer * share : (peer + 1) * share]
        out_ref[peer, pl.ds(share, height - share), :] = named.astype(jnp.bfloat16)


def first(tile_block, pieces, peers):
    rank = pieces.shape[-1]
    return pl.pallas_call(
        first_kernel,
        out_shape=jax.ShapeDtypeStruct((peers, rank // peers + NAME_ROWS, rank), pieces.dtype),
        in_specs=[SCALARS, WHOLE],
        out_specs=WHOLE,
        compiler_params=pltpu.CompilerParams(vmem_limit_bytes=VMEM_BYTES),
    )(tile_block, pieces)


def pick_kernel(wanted_ref, pieces_ref, grams_ref, out_ref):
    peers, height, rank = out_ref.shape
    share = rank // peers
    piece = pieces_ref.shape[1]
    slots = (height - share) // piece
    gram = jnp.sum(grams_ref[:, pl.ds(0, share), :].astype(jnp.float32), axis=0)
    gram = gram.astype(jnp.bfloat16)
    for peer in range(peers):
        for slot in range(slots):
            out_ref[peer, pl.ds(slot * piece, piece), :] = pieces_ref[wanted_ref[peer, slot]]
        out_ref[peer, pl.ds(slots * piece, share), :] = gram


def pick(wanted, pieces, grams, slots):
    peers = wanted.shape[0]
    _, piece, rank = pieces.shape
    return pl.pallas_call(
        pick_kernel,
        out_shape=jax.ShapeDtypeStruct((peers, slots * piece + rank // peers, rank), pieces.dtype),
        in_specs=[SCALARS, WHOLE, WHOLE],
        out_specs=WHOLE,
        compiler_params=pltpu.CompilerParams(vmem_limit_bytes=VMEM_BYTES),
    )(wanted, pieces, grams)


def hold_kernel(tiles_ref, held_ref, arrived):
    copy = pltpu.make_async_copy(tiles_ref, held_ref, arrived)
    copy.start()
    copy.wait()


def hold(tiles):
    return pl.pallas_call(
        hold_kernel,
        out_shape=jax.ShapeDtypeStruct(tiles.shape, tiles.dtype),
        in_specs=[FAR],
        out_specs=WHOLE,
        scratch_shapes=[pltpu.SemaphoreType.DMA],
        compiler_params=pltpu.CompilerParams(vmem_limit_bytes=VMEM_BYTES),
        cost_estimate=pl.CostEstimate(flops=0, transcendentals=0, bytes_accessed=4 * tiles.size),
    )(tiles)


def tile_kernel(with_direction, count_ref, tiles_ref, factors_ref, *refs):
    if with_direction:
        left_ref, out_ref, total_ref = refs
    else:
        out_ref, total_ref = refs
    slots = tiles_ref.shape[0]
    rows, rank = total_ref.shape
    piece = rows // factors_ref.shape[0]
    step = min(ROW_CHUNK, rows)

    if with_direction:
        share = factors_ref.shape[1] - slots * piece
        gram = factors_ref[:, pl.ds(slots * piece, share), :].reshape(rank, rank)
        total_ref[...] = jnp.dot(left_ref[...], gram, preferred_element_type=jnp.float32)
    else:
        total_ref[...] = jnp.zeros_like(total_ref)

    for slot in range(slots):

        @pl.when(slot < count_ref[0, 0])
        def add():
            factors = factors_ref[:, pl.ds(slot * piece, piece), :].reshape(rows, rank)
            for at in range(0, rows, step):
                chunk = pl.ds(at, step)
                values = tiles_ref[slot, chunk, :].astype(jnp.float32)
                if with_direction:
                    scores = lax.dot_general(
                        left_ref[chunk, :],
                        factors,
                        (((1,), (1,)), ((), ())),
                        preferred_element_type=jnp.float32,
                    )
                    weighted = (values * scores).astype(jnp.bfloat16)
                else:
                    weighted = (1.0 + values).astype(jnp.bfloat16)
                total_ref[chunk, :] += jnp.dot(
                    weighted, factors, preferred_element_type=jnp.float32
                )

    encode(total_ref, out_ref)


def encode(total_ref, out_ref):
    owners = out_ref.shape[0]
    share = total_ref.shape[0] // owners
    for owner in range(owners):
        block = total_ref[pl.ds(owner * share, share), :]
        largest = jnp.max(jnp.abs(block), axis=(0, 1), keepdims=True)
        level = jnp.ceil(jnp.log(jnp.maximum(largest, 1e-30)) * SCALE_STEPS)
        whole = jnp.round(block * (FULL_SCALE * jnp.exp(level * (-1.0 / SCALE_STEPS))))
        whole = whole.astype(jnp.int32).astype(jnp.int16)
        for at in range(0, block.shape[1], LANES):
            out_ref[owner, pl.ds(at // LANES * share, share), :] = whole[:, at : at + LANES]
        out_ref[owner, pl.ds(out_ref.shape[1] - SCALE_ROWS, SCALE_ROWS), :] = jnp.broadcast_to(
            level.astype(jnp.int32), (SCALE_ROWS, LANES)
        ).astype(jnp.int16)


def decode(parts, share, rank):
    levels = parts[:, -1:, :1].astype(jnp.float32)
    values = parts[:, : share * rank // LANES].astype(jnp.float32)
    total = jnp.sum(values * (jnp.exp(levels * (1.0 / SCALE_STEPS)) * (1.0 / FULL_SCALE)), axis=0)
    return jnp.concatenate([total[at : at + share] for at in range(0, total.shape[0], share)], axis=1)


def tile_sum(owners, tile_count, tiles, factors, left=None):
    slots, rows, items = tiles.shape
    rank = factors.shape[-1]
    extra = () if left is None else (left,)
    return pl.pallas_call(
        functools.partial(tile_kernel, left is not None),
        out_shape=jax.ShapeDtypeStruct(
            (owners, rows // owners * rank // LANES + SCALE_ROWS, LANES), jnp.int16
        ),
        in_specs=[SCALARS, WHOLE, WHOLE] + [WHOLE] * len(extra),
        out_specs=WHOLE,
        scratch_shapes=[
            pltpu.VMEM((rows, rank), jnp.float32),
        ],
        compiler_params=pltpu.CompilerParams(vmem_limit_bytes=VMEM_BYTES),
    )(tile_count, tiles, factors, *extra)


def exchange(parts, axes):
    return lax.all_to_all(parts, axes, 0, 0, tiled=True)


def gather(block, axes):
    size = lax.axis_size(axes)
    return exchange(jnp.broadcast_to(block[None], (size,) + block.shape), axes)


def shards(confidence, tile_block, tile_count, item_factors):
    tiles = hold(confidence[0, 0])
    slots, rows, _ = tiles.shape
    rank = item_factors.shape[1]
    owners = lax.axis_size(ITEMS)

    peers = lax.axis_size("x")
    share = rank // peers
    pieces = gather(item_factors, "z")
    grams = exchange(first(tile_block, pieces, peers), "x")
    wanted = grams[:, share, :LANES].astype(jnp.int32)
    factors = exchange(pick(wanted, pieces, grams, slots), "x")

    def reduce_rows(coded):
        return decode(exchange(coded, ITEMS), rows // owners, rank)

    right_side = reduce_rows(tile_sum(owners, tile_count, tiles, factors))
    solution = jnp.zeros_like(right_side)
    residual = right_side
    direction = right_side
    norm_now = jnp.sum(residual * residual, axis=1, keepdims=True)
    for step in range(STEPS):
        left = gather(direction.astype(jnp.bfloat16), ITEMS).reshape(rows, rank)
        image = (
            reduce_rows(tile_sum(owners, tile_count, tiles, factors, left))
            + DAMPING * direction
        )
        step_size = norm_now / jnp.sum(direction * image, axis=1, keepdims=True)
        solution = solution + step_size * direction
        residual = residual - step_size * image
        norm_next = jnp.sum(residual * residual, axis=1, keepdims=True)
        direction = residual + norm_next / norm_now * direction
        norm_now = norm_next
    return (solution, residual)


def solution(mesh):
    chips = Mesh(mesh.devices.reshape(8, 8, 8, 2), USERS + ITEMS)
    in_specs = (
        P(USERS, ITEMS, None, None, None),
        P(USERS, ITEMS, None),
        P(USERS, ITEMS),
        P(ITEMS + USERS, None),
    )
    out_specs = (P(USERS + ITEMS, None), P(USERS + ITEMS, None))
    return jax.shard_map(shards, mesh=chips, in_specs=in_specs, out_specs=out_specs, check_vma=False)
```

time: 167 us -> 164 us (0.982)
  blocking collectives: 99.8 us -> 128 us
  starting transfers between devices: 20.1 us -> 3.55 us
  waiting for transfers between devices: 33.5 us -> 20.7 us
  local copies, waits for them, and re-layouts: 0.85 us -> 2.9 us
  Pallas kernels: 6.83 us -> 5.11 us
    all_to_all x6 -> x7, blocking collectives: 99.8 us -> 128 us  [exchange(): return lax.all_to_all(parts, axes, 0, 0, tiled=True)]
    all_to_all x2 -> x1, starting transfers between devices: 20.1 us -> 3.55 us  [exchange(): return lax.all_to_all(parts, axes, 0, 0, tiled=True)]
    all_to_all x2 -> x1, waiting for transfers between devices: 33.5 us -> 20.7 us  [exchange(): return lax.all_to_all(parts, axes, 0, 0, tiled=True)]
    pallas_call x3, Pallas kernels: 4.47 us -> 2.59 us  [tile_sum(): pl.pallas_call(functools.partial(tile_kernel, left is not None), out_shap...]
  transfers between devices with their start and end apart: 2 -> 1, of which waited for: 2 -> 1; matrix products, arithmetic and copies ran while one was open for 0% -> 0% of each run, Pallas kernels for 0% -> 0%
where the time goes in v3:
time: 164 us
  blocking collectives  128 us (78%)
  waiting for transfers between devices  20.7 us (13%)
  Pallas kernels  5.11 us (3%)
  starting transfers between devices  3.55 us (2%)
  local copies, waits for them, and re-layouts  2.9 us (2%)
  other arithmetic  2.33 us (1%)
    all_to_all x7, blocking collectives, exchange(): return lax.all_to_all(parts, axes, 0, 0, tiled=True)  128 us
    all_to_all x1, waiting for transfers between devices, exchange(): return lax.all_to_all(parts, axes, 0, 0, tiled=True)  20.7 us
    all_to_all x1, starting transfers between devices, exchange(): return lax.all_to_all(parts, axes, 0, 0, tiled=True)  3.55 us
  transfers between devices with their start and end apart: 1, of which 1 were waited for; matrix products, arithmetic and copies ran while one was open for 0% of the time, Pallas kernels for 0%

profile of v3, /device:TPU:1, one launch (start us, length us, event | category | flops | bytes accessed | tf_op | source)
XLA Modules:
  0.0 163.6 jit_solution(34652090689491401)
XLA Ops:
  0.6 0.8 broadcast_in_dim.6
  1.4 27.4 %all_to_all.40.pieces_ref = bf16[8,64,256]{2,1,0:T(8,128)(2,1)S(1)} all-to-all(bf16[8,64,256]{2,1,0:T(8,128)(2,1)S(1)} %broadcast_in_dim.6), channel_id=1, replica_groups=mesh['z'=8,'x'=8,'y'=8,'core'=2] {'z'}, dimensions={0} | all-to-all | bytes 524288 | tf_op jit(solution)/shard_map/all_to_all | solution.py:182
  28.8 0.7 copy-done.1
  29.5 0.8 shard_map.60
  30.3 14.7 %all_to_all.41.grams_ref = bf16[8,40,256]{2,1,0:T(8,128)(2,1)S(1)} all-to-all(bf16[8,40,256]{2,1,0:T(8,128)(2,1)S(1)} %shard_map.60), channel_id=1, replica_groups=mesh['z'=8,'x'=8,'y'=8,'core'=2] {'x'}, dimensions={0} | all-to-all | bytes 327680 | tf_op jit(solution)/shard_map/all_to_all | solution.py:182
  44.9 1.6 shard_map.61
  46.5 3.6 %all-to-all-start.2 = ((bf16[8,224,256]{2,1,0:T(8,128)(2,1)}), bf16[8,224,256]{2,1,0:T(8,128)(2,1)S(1)}, u32[]{:S(2)}, u32[]{:S(2)}) async-start(bf16[8,224,256]{2,1,0:T(8,128)(2,1)} %shard_map.61), calls=%async_computation.2 | async-start | bytes 1835008 | tf_op jit(solution)/shard_map/all_to_all | solution.py:182
  50.8 1.4 copy-done
  52.3 20.7 %all-to-all-done.2.factors_ref = bf16[8,224,256]{2,1,0:T(8,128)(2,1)S(1)} async-done(((bf16[8,224,256]{2,1,0:T(8,128)(2,1)}), bf16[8,224,256]{2,1,0:T(8,128)(2,1)S(1)}, u32[]{:S(2)}, u32[]{:S(2)}) %all-to-all-start.2) | async-done | bytes 917536 | tf_op jit(solution)/shard_map/all_to_all | solution.py:182
  73.0 0.5 shard_map.62
  73.5 24.3 %all_to_all.42 = s16[16,72,128]{2,1,0:T(8,128)(2,1)S(1)} all-to-all(s16[16,72,128]{2,1,0:T(8,128)(2,1)S(1)} %shard_map.62), channel_id=1, replica_groups=mesh['z'=8,'x'=8,'y'=8,'core'=2] {'y','core'}, dimensions={0} | all-to-all | bytes 589824 | tf_op jit(solution)/shard_map/all_to_all | solution.py:182
  97.8 0.2 fusion.9
  98.1 0.1 multiply_reduce_fusion.2
  98.2 14.4 %all_to_all.43 = bf16[16,32,256]{2,1,0:T(8,128)(2,1)S(1)} all-to-all(bf16[16,32,256]{2,1,0:T(8,128)(2,1)S(1)} %broadcast_in_dim.7), channel_id=1, replica_groups=mesh['z'=8,'x'=8,'y'=8,'core'=2] {'y','core'}, dimensions={0} | all-to-all | bytes 524288 | tf_op jit(solution)/shard_map/all_to_all | solution.py:182
  112.7 1.0 shard_map.63
  113.7 16.2 %all_to_all.44 = s16[16,72,128]{2,1,0:T(8,128)(2,1)S(1)} all-to-all(s16[16,72,128]{2,1,0:T(8,128)(2,1)S(1)} %shard_map.63), channel_id=1, replica_groups=mesh['z'=8,'x'=8,'y'=8,'core'=2] {'y','core'}, dimensions={0} | all-to-all | bytes 589824 | tf_op jit(solution)/shard_map/all_to_all | solution.py:182
  129.9 0.2 fusion.10
  130.4 0.2 multiply_reduce_fusion.4
  130.7 14.4 %all_to_all.45 = bf16[16,32,256]{2,1,0:T(8,128)(2,1)S(1)} all-to-all(bf16[16,32,256]{2,1,0:T(8,128)(2,1)S(1)} %broadcast_in_dim.8), channel_id=1, replica_groups=mesh['z'=8,'x'=8,'y'=8,'core'=2] {'y','core'}, dimensions={0} | all-to-all | bytes 524288 | tf_op jit(solution)/shard_map/all_to_all | solution.py:182
  145.1 1.0 shard_map.64
  146.2 16.2 %all_to_all.46 = s16[16,72,128]{2,1,0:T(8,128)(2,1)S(1)} all-to-all(s16[16,72,128]{2,1,0:T(8,128)(2,1)S(1)} %shard_map.64), channel_id=1, replica_groups=mesh['z'=8,'x'=8,'y'=8,'core'=2] {'y','core'}, dimensions={0} | all-to-all | bytes 589824 | tf_op jit(solution)/shard_map/all_to_all | solution.py:182
  162.4 0.2 fusion.11
  162.7 0.2 multiply_reduce_fusion.3
  162.9 0.7 multiply_subtract_fusion
  (17 shorter events, 0.6 us)
Async XLA Ops:
  28.8 0.7 copy-start.1
  46.5 26.4 %all-to-all-start.2 = ((bf16[8,224,256]{2,1,0:T(8,128)(2,1)}), bf16[8,224,256]{2,1,0:T(8,128)(2,1)S(1)}, u32[]{:S(2)}, u32[]{:S(2)}) async-start(bf16[8,224,256]{2,1,0:T(8,128)(2,1)} %shard_map.61), calls=%async_computation.2 | async-start | bytes 1835008 | tf_op jit(solution)/shard_map/all_to_all | solution.py:182
  50.7 1.4 copy-start

commit v4 on v3

--- a/solution.py
+++ b/solution.py
@@ -24,44 +24,50 @@
 FAR = pl.BlockSpec(memory_space=pltpu.HBM)
 
 
-def first_kernel(blocks_ref, pieces_ref, out_ref):
+def first_kernel(names_ref, pieces_ref, out_ref):
     peers, height, rank = out_ref.shape
     share = rank // peers
-    slots = blocks_ref.shape[2]
     flat = pieces_ref[...].reshape(-1, rank)
     gram = lax.dot_general(
         flat, flat, (((0,), (0,)), ((), ())), preferred_element_type=jnp.float32
     ).astype(jnp.bfloat16)
-    lane = lax.broadcasted_iota(jnp.int32, (height - share, rank), 1)
-    named = jnp.zeros((height - share, rank), jnp.float32)
-    for slot in range(slots):
-        named = jnp.where(lane == slot, blocks_ref[0, 0, slot].astype(jnp.float32), named)
+    names = names_ref[...]
     for peer in range(peers):
         out_ref[peer, pl.ds(0, share), :] = gram[peer * share : (peer + 1) * share]
-        out_ref[peer, pl.ds(share, height - share), :] = named.astype(jnp.bfloat16)
-
-
-def first(tile_block, pieces, peers):
+        out_ref[peer, pl.ds(share, height - share), :] = names
+
+
+def first(names, pieces, peers):
     rank = pieces.shape[-1]
     return pl.pallas_call(
         first_kernel,
         out_shape=jax.ShapeDtypeStruct((peers, rank // peers + NAME_ROWS, rank), pieces.dtype),
-        in_specs=[SCALARS, WHOLE],
-        out_specs=WHOLE,
-        compiler_params=pltpu.CompilerParams(vmem_limit_bytes=VMEM_BYTES),
-    )(tile_block, pieces)
+        in_specs=[WHOLE, WHOLE],
+        out_specs=WHOLE,
+        compiler_params=pltpu.CompilerParams(vmem_limit_bytes=VMEM_BYTES),
+    )(names, pieces)
 
 
 def pick_kernel(wanted_ref, pieces_ref, grams_ref, out_ref):
     peers, height, rank = out_ref.shape
     share = rank // peers
-    piece = pieces_ref.shape[1]
+    blocks, piece, _ = pieces_ref.shape
     slots = (height - share) // piece
     gram = jnp.sum(grams_ref[:, pl.ds(0, share), :].astype(jnp.float32), axis=0)
     gram = gram.astype(jnp.bfloat16)
     for peer in range(peers):
         for slot in range(slots):
-            out_ref[peer, pl.ds(slot * piece, piece), :] = pieces_ref[wanted_ref[peer, slot]]
+            name = wanted_ref[peer, slot]
+            rows = pl.ds(slot * piece, piece)
+
+            @pl.when(name < blocks)
+            def live():
+                out_ref[peer, rows, :] = pieces_ref[name]
+
+            @pl.when(name >= blocks)
+            def dead():
+                out_ref[peer, rows, :] = jnp.zeros((piece, rank), out_ref.dtype)
+
         out_ref[peer, pl.ds(slots * piece, share), :] = gram
 
 
@@ -95,7 +101,7 @@
     )(tiles)
 
 
-def tile_kernel(with_direction, count_ref, tiles_ref, factors_ref, *refs):
+def tile_kernel(with_direction, tiles_ref, factors_ref, *refs):
     if with_direction:
         left_ref, out_ref, total_ref = refs
     else:
@@ -104,36 +110,28 @@
     rows, rank = total_ref.shape
     piece = rows // factors_ref.shape[0]
     step = min(ROW_CHUNK, rows)
-
     if with_direction:
         share = factors_ref.shape[1] - slots * piece
         gram = factors_ref[:, pl.ds(slots * piece, share), :].reshape(rank, rank)
-        total_ref[...] = jnp.dot(left_ref[...], gram, preferred_element_type=jnp.float32)
-    else:
-        total_ref[...] = jnp.zeros_like(total_ref)
-
-    for slot in range(slots):
-
-        @pl.when(slot < count_ref[0, 0])
-        def add():
+    for at in range(0, rows, step):
+        chunk = pl.ds(at, step)
+        if with_direction:
+            left = left_ref[chunk, :]
+            total = jnp.dot(left, gram, preferred_element_type=jnp.float32)
+        else:
+            total = jnp.zeros((step, rank), jnp.float32)
+        for slot in range(slots):
             factors = factors_ref[:, pl.ds(slot * piece, piece), :].reshape(rows, rank)
-            for at in range(0, rows, step):
-                chunk = pl.ds(at, step)
-                values = tiles_ref[slot, chunk, :].astype(jnp.float32)
-                if with_direction:
-                    scores = lax.dot_general(
-                        left_ref[chunk, :],
-                        factors,
-                        (((1,), (1,)), ((), ())),
-                        preferred_element_type=jnp.float32,
-                    )
-                    weighted = (values * scores).astype(jnp.bfloat16)
-                else:
-                    weighted = (1.0 + values).astype(jnp.bfloat16)
-                total_ref[chunk, :] += jnp.dot(
-                    weighted, factors, preferred_element_type=jnp.float32
+            values = tiles_ref[slot, chunk, :].astype(jnp.float32)
+            if with_direction:
+                scores = lax.dot_general(
+                    left, factors, (((1,), (1,)), ((), ())), preferred_element_type=jnp.float32
                 )
-
+                weighted = (values * scores).astype(jnp.bfloat16)
+            else:
+                weighted = (1.0 + values).astype(jnp.bfloat16)
+            total += jnp.dot(weighted, factors, preferred_element_type=jnp.float32)
+        total_ref[chunk, :] = total
     encode(total_ref, out_ref)
 
 
@@ -160,7 +158,7 @@
     return jnp.concatenate([total[at : at + share] for at in range(0, total.shape[0], share)], axis=1)
 
 
-def tile_sum(owners, tile_count, tiles, factors, left=None):
+def tile_sum(owners, tiles, factors, left=None):
     slots, rows, items = tiles.shape
     rank = factors.shape[-1]
     extra = () if left is None else (left,)
@@ -169,13 +167,13 @@
         out_shape=jax.ShapeDtypeStruct(
             (owners, rows // owners * rank // LANES + SCALE_ROWS, LANES), jnp.int16
         ),
-        in_specs=[SCALARS, WHOLE, WHOLE] + [WHOLE] * len(extra),
+        in_specs=[WHOLE, WHOLE] + [WHOLE] * len(extra),
         out_specs=WHOLE,
         scratch_shapes=[
             pltpu.VMEM((rows, rank), jnp.float32),
         ],
         compiler_params=pltpu.CompilerParams(vmem_limit_bytes=VMEM_BYTES),
-    )(tile_count, tiles, factors, *extra)
+    )(tiles, factors, *extra)
 
 
 def exchange(parts, axes):
@@ -196,14 +194,18 @@
     peers = lax.axis_size("x")
     share = rank // peers
     pieces = gather(item_factors, "z")
-    grams = exchange(first(tile_block, pieces, peers), "x")
+    live = jnp.arange(slots, dtype=jnp.int32)[None] < tile_count
+    names = jnp.where(live, tile_block[0], lax.axis_size("z")).astype(jnp.bfloat16)
+    names = jnp.pad(names, ((0, 0), (0, rank - slots)))
+    names = jnp.broadcast_to(names, (NAME_ROWS, rank))
+    grams = exchange(first(names, pieces, peers), "x")
     wanted = grams[:, share, :LANES].astype(jnp.int32)
     factors = exchange(pick(wanted, pieces, grams, slots), "x")
 
     def reduce_rows(coded):
         return decode(exchange(coded, ITEMS), rows // owners, rank)
 
-    right_side = reduce_rows(tile_sum(owners, tile_count, tiles, factors))
+    right_side = reduce_rows(tile_sum(owners, tiles, factors))
     solution = jnp.zeros_like(right_side)
     residual = right_side
     direction = right_side
@@ -211,7 +213,7 @@
     for step in range(STEPS):
         left = gather(direction.astype(jnp.bfloat16), ITEMS).reshape(rows, rank)
         image = (
-            reduce_rows(tile_sum(owners, tile_count, tiles, factors, left))
+            reduce_rows(tile_sum(owners, tiles, factors, left))
             + DAMPING * direction
         )
         step_size = norm_now / jnp.sum(direction * image, axis=1, keepdims=True)

time: 164 us -> 162 us (0.988)
  blocking collectives: 128 us -> 97.3 us
  starting transfers between devices: 3.55 us -> 20.8 us
  waiting for transfers between devices: 20.7 us -> 30.4 us
    all_to_all x7 -> x6, blocking collectives: 128 us -> 97.3 us  [exchange(): return lax.all_to_all(parts, axes, 0, 0, tiled=True)]
    all_to_all x1 -> x2, starting transfers between devices: 3.55 us -> 20.8 us  [exchange(): return lax.all_to_all(parts, axes, 0, 0, tiled=True)]
    all_to_all x1 -> x2, waiting for transfers between devices: 20.7 us -> 30.4 us  [exchange(): return lax.all_to_all(parts, axes, 0, 0, tiled=True)]
  transfers between devices with their start and end apart: 1 -> 2, of which waited for: 1 -> 2; matrix products, arithmetic and copies ran while one was open for 0% -> 0% of each run, Pallas kernels for 0% -> 0%
where the time goes in v4:
time: 162 us
  blocking collectives  97.3 us (60%)
  waiting for transfers between devices  30.4 us (19%)
  starting transfers between devices  20.8 us (13%)
  Pallas kernels  5.78 us (4%)
  other arithmetic  2.99 us (2%)
  local copies, waits for them, and re-layouts  2.96 us (2%)
    all_to_all x6, blocking collectives, exchange(): return lax.all_to_all(parts, axes, 0, 0, tiled=True)  97.3 us
    all_to_all x2, waiting for transfers between devices, exchange(): return lax.all_to_all(parts, axes, 0, 0, tiled=True)  30.4 us
    all_to_all x2, starting transfers between devices, exchange(): return lax.all_to_all(parts, axes, 0, 0, tiled=True)  20.8 us
    pallas_call x3, Pallas kernels, tile_sum(): pl.pallas_call(functools.partial(tile_kernel, left is not None), out_shap...  3.55 us
  transfers between devices with their start and end apart: 2, of which 2 were waited for; matrix products, arithmetic and copies ran while one was open for 0% of the time, Pallas kernels for 0%

profile of v4, /device:TPU:1, one launch (start us, length us, event | category | flops | bytes accessed | tf_op | source)
XLA Modules:
  0.0 161.6 jit_solution(8569303817401500679)
XLA Ops:
  0.6 1.5 broadcast_in_dim.17
  2.1 17.2 %all-to-all-start = ((bf16[8,64,256]{2,1,0:T(8,128)(2,1)}), bf16[8,64,256]{2,1,0:T(8,128)(2,1)S(1)}, u32[]{:S(2)}, u32[]{:S(2)}) async-start(bf16[8,64,256]{2,1,0:T(8,128)(2,1)} %broadcast_in_dim.17), calls=%async_computation | async-start | bytes 524288 | tf_op jit(solution)/shard_map/all_to_all | solution.py:180
  20.0 0.7 fusion.13
  20.7 9.0 %all-to-all-done.pieces_ref = bf16[8,64,256]{2,1,0:T(8,128)(2,1)S(1)} async-done(((bf16[8,64,256]{2,1,0:T(8,128)(2,1)}), bf16[8,64,256]{2,1,0:T(8,128)(2,1)S(1)}, u32[]{:S(2)}, u32[]{:S(2)}) %all-to-all-start) | async-done | bytes 262176 | tf_op jit(solution)/shard_map/all_to_all | solution.py:180
  29.7 0.3 shard_map.60
  30.0 14.7 %all_to_all.40.grams_ref = bf16[8,40,256]{2,1,0:T(8,128)(2,1)S(1)} all-to-all(bf16[8,40,256]{2,1,0:T(8,128)(2,1)S(1)} %shard_map.60), channel_id=1, replica_groups=mesh['z'=8,'x'=8,'y'=8,'core'=2] {'x'}, dimensions={0} | all-to-all | bytes 327680 | tf_op jit(solution)/shard_map/all_to_all | solution.py:180
  44.6 1.8 %shard_map.61 = bf16[8,224,256]{2,1,0:T(8,128)(2,1)} custom-call(s32[8,128]{1,0:T(8,128)S(1)} %bitcast.11, bf16[8,64,256]{2,1,0:T(8,128)(2,1)S(1)} %all-to-all-done.pieces_ref, bf16[8,40,256]{2,1,0:T(8,128)(2,1)S(1)} %all_to_all.40.grams_ref), custom_call_target="tpu_custom_call" | custom-call | tf_op jit(solution)/shard_map/pallas_call | solution.py:77
  46.5 3.6 %all-to-all-start.2 = ((bf16[8,224,256]{2,1,0:T(8,128)(2,1)}), bf16[8,224,256]{2,1,0:T(8,128)(2,1)S(1)}, u32[]{:S(2)}, u32[]{:S(2)}) async-start(bf16[8,224,256]{2,1,0:T(8,128)(2,1)} %shard_map.61), calls=%async_computation.2 | async-start | bytes 1835008 | tf_op jit(solution)/shard_map/all_to_all | solution.py:180
  50.1 1.4 copy-done
  51.6 21.3 %all-to-all-done.2.factors_ref = bf16[8,224,256]{2,1,0:T(8,128)(2,1)S(1)} async-done(((bf16[8,224,256]{2,1,0:T(8,128)(2,1)}), bf16[8,224,256]{2,1,0:T(8,128)(2,1)S(1)}, u32[]{:S(2)}, u32[]{:S(2)}) %all-to-all-start.2) | async-done | bytes 917536 | tf_op jit(solution)/shard_map/all_to_all | solution.py:180
  72.9 0.8 shard_map.62
  73.7 23.7 %all_to_all.41 = s16[16,72,128]{2,1,0:T(8,128)(2,1)S(1)} all-to-all(s16[16,72,128]{2,1,0:T(8,128)(2,1)S(1)} %shard_map.62), channel_id=1, replica_groups=mesh['z'=8,'x'=8,'y'=8,'core'=2] {'y','core'}, dimensions={0} | all-to-all | bytes 589824 | tf_op jit(solution)/shard_map/all_to_all | solution.py:180
  97.4 0.2 fusion.9
  97.8 14.4 %all_to_all.42 = bf16[16,32,256]{2,1,0:T(8,128)(2,1)S(1)} all-to-all(bf16[16,32,256]{2,1,0:T(8,128)(2,1)S(1)} %broadcast_in_dim.18), channel_id=1, replica_groups=mesh['z'=8,'x'=8,'y'=8,'core'=2] {'y','core'}, dimensions={0} | all-to-all | bytes 524288 | tf_op jit(solution)/shard_map/all_to_all | solution.py:180
  112.2 1.4 shard_map.63
  113.6 15.1 %all_to_all.43 = s16[16,72,128]{2,1,0:T(8,128)(2,1)S(1)} all-to-all(s16[16,72,128]{2,1,0:T(8,128)(2,1)S(1)} %shard_map.63), channel_id=1, replica_groups=mesh['z'=8,'x'=8,'y'=8,'core'=2] {'y','core'}, dimensions={0} | all-to-all | bytes 589824 | tf_op jit(solution)/shard_map/all_to_all | solution.py:180
  128.7 0.2 fusion.10
  129.2 0.2 multiply_reduce_fusion.4
  129.5 14.4 %all_to_all.44 = bf16[16,32,256]{2,1,0:T(8,128)(2,1)S(1)} all-to-all(bf16[16,32,256]{2,1,0:T(8,128)(2,1)S(1)} %broadcast_in_dim.19), channel_id=1, replica_groups=mesh['z'=8,'x'=8,'y'=8,'core'=2] {'y','core'}, dimensions={0} | all-to-all | bytes 524288 | tf_op jit(solution)/shard_map/all_to_all | solution.py:180
  143.9 1.4 shard_map.64
  145.3 15.1 %all_to_all.45 = s16[16,72,128]{2,1,0:T(8,128)(2,1)S(1)} all-to-all(s16[16,72,128]{2,1,0:T(8,128)(2,1)S(1)} %shard_map.64), channel_id=1, replica_groups=mesh['z'=8,'x'=8,'y'=8,'core'=2] {'y','core'}, dimensions={0} | all-to-all | bytes 589824 | tf_op jit(solution)/shard_map/all_to_all | solution.py:180
  160.4 0.2 fusion.11
  160.7 0.2 multiply_reduce_fusion.3
  160.9 0.7 multiply_subtract_fusion
  (19 shorter events, 0.8 us)
Async XLA Ops:
  2.1 27.6 %all-to-all-start = ((bf16[8,64,256]{2,1,0:T(8,128)(2,1)}), bf16[8,64,256]{2,1,0:T(8,128)(2,1)S(1)}, u32[]{:S(2)}, u32[]{:S(2)}) async-start(bf16[8,64,256]{2,1,0:T(8,128)(2,1)} %broadcast_in_dim.17), calls=%async_computation | async-start | bytes 524288 | tf_op jit(solution)/shard_map/all_to_all | solution.py:180
  46.5 26.4 %all-to-all-start.2 = ((bf16[8,224,256]{2,1,0:T(8,128)(2,1)}), bf16[8,224,256]{2,1,0:T(8,128)(2,1)S(1)}, u32[]{:S(2)}, u32[]{:S(2)}) async-start(bf16[8,224,256]{2,1,0:T(8,128)(2,1)} %shard_map.61), calls=%async_computation.2 | async-start | bytes 1835008 | tf_op jit(solution)/shard_map/all_to_all | solution.py:180
  50.1 1.4 copy-start

commit v5 on v4

--- a/solution.py
+++ b/solution.py
@@ -13,8 +13,8 @@
 ROW_CHUNK = 256
 VMEM_BYTES = 24 * 1024 * 1024
 LANES = 128
-SCALE_ROWS = 8
-NAME_ROWS = 8
+SCALE_ROWS = 16
+NAME_ROWS = 16
 SCALE_STEPS = 64.0
 FULL_SCALE = 32000.0
 USERS = ("z", "x")
@@ -25,23 +25,31 @@
 
 
 def first_kernel(names_ref, pieces_ref, out_ref):
-    peers, height, rank = out_ref.shape
+    peers = out_ref.shape[0]
+    rank = pieces_ref.shape[2]
     share = rank // peers
+    strips = rank // LANES
     flat = pieces_ref[...].reshape(-1, rank)
     gram = lax.dot_general(
         flat, flat, (((0,), (0,)), ((), ())), preferred_element_type=jnp.float32
     ).astype(jnp.bfloat16)
     names = names_ref[...]
     for peer in range(peers):
-        out_ref[peer, pl.ds(0, share), :] = gram[peer * share : (peer + 1) * share]
-        out_ref[peer, pl.ds(share, height - share), :] = names
+        rows = gram[peer * share : (peer + 1) * share]
+        for strip in range(strips):
+            out_ref[peer, pl.ds(strip * share, share), :] = rows[
+                :, strip * LANES : (strip + 1) * LANES
+            ]
+        out_ref[peer, pl.ds(strips * share, NAME_ROWS), :] = names
 
 
 def first(names, pieces, peers):
     rank = pieces.shape[-1]
     return pl.pallas_call(
         first_kernel,
-        out_shape=jax.ShapeDtypeStruct((peers, rank // peers + NAME_ROWS, rank), pieces.dtype),
+        out_shape=jax.ShapeDtypeStruct(
+            (peers, rank // peers * rank // LANES + NAME_ROWS, LANES), pieces.dtype
+        ),
         in_specs=[WHOLE, WHOLE],
         out_specs=WHOLE,
         compiler_params=pltpu.CompilerParams(vmem_limit_bytes=VMEM_BYTES),
@@ -53,8 +61,13 @@
     share = rank // peers
     blocks, piece, _ = pieces_ref.shape
     slots = (height - share) // piece
-    gram = jnp.sum(grams_ref[:, pl.ds(0, share), :].astype(jnp.float32), axis=0)
-    gram = gram.astype(jnp.bfloat16)
+    gram = jnp.concatenate(
+        [
+            jnp.sum(grams_ref[:, pl.ds(strip * share, share), :].astype(jnp.float32), axis=0)
+            for strip in range(rank // LANES)
+        ],
+        axis=1,
+    ).astype(jnp.bfloat16)
     for peer in range(peers):
         for slot in range(slots):
             name = wanted_ref[peer, slot]
@@ -192,14 +205,13 @@
     owners = lax.axis_size(ITEMS)
 
     peers = lax.axis_size("x")
-    share = rank // peers
     pieces = gather(item_factors, "z")
     live = jnp.arange(slots, dtype=jnp.int32)[None] < tile_count
     names = jnp.where(live, tile_block[0], lax.axis_size("z")).astype(jnp.bfloat16)
-    names = jnp.pad(names, ((0, 0), (0, rank - slots)))
-    names = jnp.broadcast_to(names, (NAME_ROWS, rank))
+    names = jnp.pad(names, ((0, 0), (0, LANES - slots)))
+    names = jnp.broadcast_to(names, (NAME_ROWS, LANES))
     grams = exchange(first(names, pieces, peers), "x")
-    wanted = grams[:, share, :LANES].astype(jnp.int32)
+    wanted = grams[:, -1].astype(jnp.int32)
     factors = exchange(pick(wanted, pieces, grams, slots), "x")
 
     def reduce_rows(coded):

time: 162 us -> 164 us (1.012)
  blocking collectives: 97.3 us -> 99.5 us
    all_to_all x6, blocking collectives: 97.3 us -> 99.5 us  [exchange(): return lax.all_to_all(parts, axes, 0, 0, tiled=True)]
where the time goes in v5:
time: 164 us
  blocking collectives  99.5 us (61%)
  waiting for transfers between devices  30.4 us (19%)
  starting transfers between devices  20.8 us (13%)
  Pallas kernels  5.79 us (4%)
  other arithmetic  2.99 us (2%)
  local copies, waits for them, and re-layouts  2.94 us (2%)
    all_to_all x6, blocking collectives, exchange(): return lax.all_to_all(parts, axes, 0, 0, tiled=True)  99.5 us
    all_to_all x2, waiting for transfers between devices, exchange(): return lax.all_to_all(parts, axes, 0, 0, tiled=True)  30.4 us
    all_to_all x2, starting transfers between devices, exchange(): return lax.all_to_all(parts, axes, 0, 0, tiled=True)  20.8 us
    pallas_call x3, Pallas kernels, tile_sum(): pl.pallas_call(functools.partial(tile_kernel, left is not None), out_shap...  3.56 us
  transfers between devices with their start and end apart: 2, of which 2 were waited for; matrix products, arithmetic and copies ran while one was open for 0% of the time, Pallas kernels for 0%

profile of v5, /device:TPU:1, one launch (start us, length us, event | category | flops | bytes accessed | tf_op | source)
XLA Modules:
  0.0 163.8 jit_solution(2207470763798295784)
XLA Ops:
  0.6 1.5 broadcast_in_dim.17
  2.1 17.2 %all-to-all-start = ((bf16[8,64,256]{2,1,0:T(8,128)(2,1)}), bf16[8,64,256]{2,1,0:T(8,128)(2,1)S(1)}, u32[]{:S(2)}, u32[]{:S(2)}) async-start(bf16[8,64,256]{2,1,0:T(8,128)(2,1)} %broadcast_in_dim.17), calls=%async_computation | async-start | bytes 524288 | tf_op jit(solution)/shard_map/all_to_all | solution.py:193
  20.0 0.7 fusion.13
  20.7 9.0 %all-to-all-done.pieces_ref = bf16[8,64,256]{2,1,0:T(8,128)(2,1)S(1)} async-done(((bf16[8,64,256]{2,1,0:T(8,128)(2,1)}), bf16[8,64,256]{2,1,0:T(8,128)(2,1)S(1)}, u32[]{:S(2)}, u32[]{:S(2)}) %all-to-all-start) | async-done | bytes 262176 | tf_op jit(solution)/shard_map/all_to_all | solution.py:193
  29.7 0.3 shard_map.60
  30.0 14.7 %all_to_all.40.grams_ref = bf16[8,80,128]{2,1,0:T(8,128)(2,1)S(1)} all-to-all(bf16[8,80,128]{2,1,0:T(8,128)(2,1)S(1)} %shard_map.60), channel_id=1, replica_groups=mesh['z'=8,'x'=8,'y'=8,'core'=2] {'x'}, dimensions={0} | all-to-all | bytes 327680 | tf_op jit(solution)/shard_map/all_to_all | solution.py:193
  44.7 1.8 %shard_map.61 = bf16[8,224,256]{2,1,0:T(8,128)(2,1)} custom-call(s32[8,128]{1,0:T(8,128)S(1)} %bitcast.13, bf16[8,64,256]{2,1,0:T(8,128)(2,1)S(1)} %all-to-all-done.pieces_ref, bf16[8,80,128]{2,1,0:T(8,128)(2,1)S(1)} %all_to_all.40.grams_ref), custom_call_target="tpu_custom_call" | custom-call | tf_op jit(solution)/shard_map/pallas_call | solution.py:90
  46.5 3.6 %all-to-all-start.2 = ((bf16[8,224,256]{2,1,0:T(8,128)(2,1)}), bf16[8,224,256]{2,1,0:T(8,128)(2,1)S(1)}, u32[]{:S(2)}, u32[]{:S(2)}) async-start(bf16[8,224,256]{2,1,0:T(8,128)(2,1)} %shard_map.61), calls=%async_computation.2 | async-start | bytes 1835008 | tf_op jit(solution)/shard_map/all_to_all | solution.py:193
  50.1 1.4 copy-done
  51.6 21.3 %all-to-all-done.2.factors_ref = bf16[8,224,256]{2,1,0:T(8,128)(2,1)S(1)} async-done(((bf16[8,224,256]{2,1,0:T(8,128)(2,1)}), bf16[8,224,256]{2,1,0:T(8,128)(2,1)S(1)}, u32[]{:S(2)}, u32[]{:S(2)}) %all-to-all-start.2) | async-done | bytes 917536 | tf_op jit(solution)/shard_map/all_to_all | solution.py:193
  72.9 0.8 shard_map.62
  73.7 24.4 %all_to_all.41 = s16[16,80,128]{2,1,0:T(8,128)(2,1)S(1)} all-to-all(s16[16,80,128]{2,1,0:T(8,128)(2,1)S(1)} %shard_map.62), channel_id=1, replica_groups=mesh['z'=8,'x'=8,'y'=8,'core'=2] {'y','core'}, dimensions={0} | all-to-all | bytes 655360 | tf_op jit(solution)/shard_map/all_to_all | solution.py:193
  98.1 0.2 fusion.9
  98.5 14.4 %all_to_all.42 = bf16[16,32,256]{2,1,0:T(8,128)(2,1)S(1)} all-to-all(bf16[16,32,256]{2,1,0:T(8,128)(2,1)S(1)} %broadcast_in_dim.18), channel_id=1, replica_groups=mesh['z'=8,'x'=8,'y'=8,'core'=2] {'y','core'}, dimensions={0} | all-to-all | bytes 524288 | tf_op jit(solution)/shard_map/all_to_all | solution.py:193
  113.0 1.4 shard_map.63
  114.3 15.8 %all_to_all.43 = s16[16,80,128]{2,1,0:T(8,128)(2,1)S(1)} all-to-all(s16[16,80,128]{2,1,0:T(8,128)(2,1)S(1)} %shard_map.63), channel_id=1, replica_groups=mesh['z'=8,'x'=8,'y'=8,'core'=2] {'y','core'}, dimensions={0} | all-to-all | bytes 655360 | tf_op jit(solution)/shard_map/all_to_all | solution.py:193
  130.1 0.2 fusion.10
  130.6 0.2 multiply_reduce_fusion.4
  130.9 14.4 %all_to_all.44 = bf16[16,32,256]{2,1,0:T(8,128)(2,1)S(1)} all-to-all(bf16[16,32,256]{2,1,0:T(8,128)(2,1)S(1)} %broadcast_in_dim.19), channel_id=1, replica_groups=mesh['z'=8,'x'=8,'y'=8,'core'=2] {'y','core'}, dimensions={0} | all-to-all | bytes 524288 | tf_op jit(solution)/shard_map/all_to_all | solution.py:193
  145.4 1.4 shard_map.64
  146.7 15.8 %all_to_all.45 = s16[16,80,128]{2,1,0:T(8,128)(2,1)S(1)} all-to-all(s16[16,80,128]{2,1,0:T(8,128)(2,1)S(1)} %shard_map.64), channel_id=1, replica_groups=mesh['z'=8,'x'=8,'y'=8,'core'=2] {'y','core'}, dimensions={0} | all-to-all | bytes 655360 | tf_op jit(solution)/shard_map/all_to_all | solution.py:193
  162.5 0.2 fusion.11
  162.9 0.2 multiply_reduce_fusion.3
  163.1 0.7 multiply_subtract_fusion
  (19 shorter events, 0.8 us)
Async XLA Ops:
  2.1 27.6 %all-to-all-start = ((bf16[8,64,256]{2,1,0:T(8,128)(2,1)}), bf16[8,64,256]{2,1,0:T(8,128)(2,1)S(1)}, u32[]{:S(2)}, u32[]{:S(2)}) async-start(bf16[8,64,256]{2,1,0:T(8,128)(2,1)} %broadcast_in_dim.17), calls=%async_computation | async-start | bytes 524288 | tf_op jit(solution)/shard_map/all_to_all | solution.py:193
  46.5 26.4 %all-to-all-start.2 = ((bf16[8,224,256]{2,1,0:T(8,128)(2,1)}), bf16[8,224,256]{2,1,0:T(8,128)(2,1)S(1)}, u32[]{:S(2)}, u32[]{:S(2)}) async-start(bf16[8,224,256]{2,1,0:T(8,128)(2,1)} %shard_map.61), calls=%async_computation.2 | async-start | bytes 1835008 | tf_op jit(solution)/shard_map/all_to_all | solution.py:193
  50.1 1.4 copy-start

commit v6 on v5

--- a/solution.py
+++ b/solution.py
@@ -14,6 +14,7 @@
 VMEM_BYTES = 24 * 1024 * 1024
 LANES = 128
 SCALE_ROWS = 16
+SENT_SCALE_ROWS = 8
 NAME_ROWS = 16
 SCALE_STEPS = 64.0
 FULL_SCALE = 32000.0
@@ -215,7 +216,8 @@
     factors = exchange(pick(wanted, pieces, grams, slots), "x")
 
     def reduce_rows(coded):
-        return decode(exchange(coded, ITEMS), rows // owners, rank)
+        sent = coded[:, : coded.shape[1] - SCALE_ROWS + SENT_SCALE_ROWS]
+        return decode(exchange(sent, ITEMS), rows // owners, rank)
 
     right_side = reduce_rows(tile_sum(owners, tiles, factors))
     solution = jnp.zeros_like(right_side)

time: 164 us -> 162 us (0.988)
  blocking collectives: 99.5 us -> 97.3 us
    all_to_all x6, blocking collectives: 99.5 us -> 97.3 us  [exchange(): return lax.all_to_all(parts, axes, 0, 0, tiled=True)]
where the time goes in v6:
time: 162 us
  blocking collectives  97.3 us (60%)
  waiting for transfers between devices  30.4 us (19%)
  starting transfers between devices  20.8 us (13%)
  Pallas kernels  5.78 us (4%)
  local copies, waits for them, and re-layouts  3.02 us (2%)
  other arithmetic  2.99 us (2%)
    all_to_all x6, blocking collectives, exchange(): return lax.all_to_all(parts, axes, 0, 0, tiled=True)  97.3 us
    all_to_all x2, waiting for transfers between devices, exchange(): return lax.all_to_all(parts, axes, 0, 0, tiled=True)  30.4 us
    all_to_all x2, starting transfers between devices, exchange(): return lax.all_to_all(parts, axes, 0, 0, tiled=True)  20.8 us
    pallas_call x3, Pallas kernels, tile_sum(): pl.pallas_call(functools.partial(tile_kernel, left is not None), out_shap...  3.55 us
  transfers between devices with their start and end apart: 2, of which 2 were waited for; matrix products, arithmetic and copies ran while one was open for 0% of the time, Pallas kernels for 0%

profile of v6, /device:TPU:1, one launch (start us, length us, event | category | flops | bytes accessed | tf_op | source)
XLA Modules:
  0.0 161.7 jit_solution(486867114895809317)
XLA Ops:
  0.6 1.5 broadcast_in_dim.17
  2.1 17.2 %all-to-all-start = ((bf16[8,64,256]{2,1,0:T(8,128)(2,1)}), bf16[8,64,256]{2,1,0:T(8,128)(2,1)S(1)}, u32[]{:S(2)}, u32[]{:S(2)}) async-start(bf16[8,64,256]{2,1,0:T(8,128)(2,1)} %broadcast_in_dim.17), calls=%async_computation | async-start | bytes 524288 | tf_op jit(solution)/shard_map/all_to_all | solution.py:194
  20.0 0.7 fusion.13
  20.7 9.0 %all-to-all-done.pieces_ref = bf16[8,64,256]{2,1,0:T(8,128)(2,1)S(1)} async-done(((bf16[8,64,256]{2,1,0:T(8,128)(2,1)}), bf16[8,64,256]{2,1,0:T(8,128)(2,1)S(1)}, u32[]{:S(2)}, u32[]{:S(2)}) %all-to-all-start) | async-done | bytes 262176 | tf_op jit(solution)/shard_map/all_to_all | solution.py:194
  29.7 0.3 shard_map.60
  30.0 14.7 %all_to_all.40.grams_ref = bf16[8,80,128]{2,1,0:T(8,128)(2,1)S(1)} all-to-all(bf16[8,80,128]{2,1,0:T(8,128)(2,1)S(1)} %shard_map.60), channel_id=1, replica_groups=mesh['z'=8,'x'=8,'y'=8,'core'=2] {'x'}, dimensions={0} | all-to-all | bytes 327680 | tf_op jit(solution)/shard_map/all_to_all | solution.py:194
  44.7 1.8 %shard_map.61 = bf16[8,224,256]{2,1,0:T(8,128)(2,1)} custom-call(s32[8,128]{1,0:T(8,128)S(1)} %bitcast.13, bf16[8,64,256]{2,1,0:T(8,128)(2,1)S(1)} %all-to-all-done.pieces_ref, bf16[8,80,128]{2,1,0:T(8,128)(2,1)S(1)} %all_to_all.40.grams_ref), custom_call_target="tpu_custom_call" | custom-call | tf_op jit(solution)/shard_map/pallas_call | solution.py:91
  46.5 3.6 %all-to-all-start.2 = ((bf16[8,224,256]{2,1,0:T(8,128)(2,1)}), bf16[8,224,256]{2,1,0:T(8,128)(2,1)S(1)}, u32[]{:S(2)}, u32[]{:S(2)}) async-start(bf16[8,224,256]{2,1,0:T(8,128)(2,1)} %shard_map.61), calls=%async_computation.2 | async-start | bytes 1835008 | tf_op jit(solution)/shard_map/all_to_all | solution.py:194
  50.1 1.4 copy-done
  51.6 21.3 %all-to-all-done.2.factors_ref = bf16[8,224,256]{2,1,0:T(8,128)(2,1)S(1)} async-done(((bf16[8,224,256]{2,1,0:T(8,128)(2,1)}), bf16[8,224,256]{2,1,0:T(8,128)(2,1)S(1)}, u32[]{:S(2)}, u32[]{:S(2)}) %all-to-all-start.2) | async-done | bytes 917536 | tf_op jit(solution)/shard_map/all_to_all | solution.py:194
  72.9 0.8 shard_map.62
  73.7 23.7 %all_to_all.41 = s16[16,72,128]{2,1,0:T(8,128)(2,1)S(1)} all-to-all(s16[16,72,128]{2,1,0:T(8,128)(2,1)S(1)} %slice.65), channel_id=1, replica_groups=mesh['z'=8,'x'=8,'y'=8,'core'=2] {'y','core'}, dimensions={0} | all-to-all | bytes 589824 | tf_op jit(solution)/shard_map/all_to_all | solution.py:194
  97.4 0.2 fusion.9
  97.8 14.4 %all_to_all.42 = bf16[16,32,256]{2,1,0:T(8,128)(2,1)S(1)} all-to-all(bf16[16,32,256]{2,1,0:T(8,128)(2,1)S(1)} %broadcast_in_dim.18), channel_id=1, replica_groups=mesh['z'=8,'x'=8,'y'=8,'core'=2] {'y','core'}, dimensions={0} | all-to-all | bytes 524288 | tf_op jit(solution)/shard_map/all_to_all | solution.py:194
  112.3 1.4 shard_map.63
  113.7 15.1 %all_to_all.43 = s16[16,72,128]{2,1,0:T(8,128)(2,1)S(1)} all-to-all(s16[16,72,128]{2,1,0:T(8,128)(2,1)S(1)} %slice.70), channel_id=1, replica_groups=mesh['z'=8,'x'=8,'y'=8,'core'=2] {'y','core'}, dimensions={0} | all-to-all | bytes 589824 | tf_op jit(solution)/shard_map/all_to_all | solution.py:194
  128.8 0.2 fusion.10
  129.2 0.2 multiply_reduce_fusion.4
  129.6 14.4 %all_to_all.44 = bf16[16,32,256]{2,1,0:T(8,128)(2,1)S(1)} all-to-all(bf16[16,32,256]{2,1,0:T(8,128)(2,1)S(1)} %broadcast_in_dim.19), channel_id=1, replica_groups=mesh['z'=8,'x'=8,'y'=8,'core'=2] {'y','core'}, dimensions={0} | all-to-all | bytes 524288 | tf_op jit(solution)/shard_map/all_to_all | solution.py:194
  144.0 1.4 shard_map.64
  145.4 15.1 %all_to_all.45 = s16[16,72,128]{2,1,0:T(8,128)(2,1)S(1)} all-to-all(s16[16,72,128]{2,1,0:T(8,128)(2,1)S(1)} %slice.75), channel_id=1, replica_groups=mesh['z'=8,'x'=8,'y'=8,'core'=2] {'y','core'}, dimensions={0} | all-to-all | bytes 589824 | tf_op jit(solution)/shard_map/all_to_all | solution.py:194
  160.5 0.2 fusion.11
  160.8 0.2 multiply_reduce_fusion.3
  161.0 0.7 multiply_subtract_fusion
  (22 shorter events, 0.9 us)
Async XLA Ops:
  2.1 27.6 %all-to-all-start = ((bf16[8,64,256]{2,1,0:T(8,128)(2,1)}), bf16[8,64,256]{2,1,0:T(8,128)(2,1)S(1)}, u32[]{:S(2)}, u32[]{:S(2)}) async-start(bf16[8,64,256]{2,1,0:T(8,128)(2,1)} %broadcast_in_dim.17), calls=%async_computation | async-start | bytes 524288 | tf_op jit(solution)/shard_map/all_to_all | solution.py:194
  46.5 26.4 %all-to-all-start.2 = ((bf16[8,224,256]{2,1,0:T(8,128)(2,1)}), bf16[8,224,256]{2,1,0:T(8,128)(2,1)S(1)}, u32[]{:S(2)}, u32[]{:S(2)}) async-start(bf16[8,224,256]{2,1,0:T(8,128)(2,1)} %shard_map.61), calls=%async_computation.2 | async-start | bytes 1835008 | tf_op jit(solution)/shard_map/all_to_all | solution.py:194
  50.1 1.4 copy-start

commit v7 on v6

--- a/solution.py
+++ b/solution.py
@@ -211,7 +211,8 @@
     names = jnp.where(live, tile_block[0], lax.axis_size("z")).astype(jnp.bfloat16)
     names = jnp.pad(names, ((0, 0), (0, LANES - slots)))
     names = jnp.broadcast_to(names, (NAME_ROWS, LANES))
-    grams = exchange(first(names, pieces, peers), "x")
+    sent = first(names, pieces, peers)
+    grams = exchange(sent[:, : sent.shape[1] - NAME_ROWS + SENT_SCALE_ROWS], "x")
     wanted = grams[:, -1].astype(jnp.int32)
     factors = exchange(pick(wanted, pieces, grams, slots), "x")
 

time: 162 us -> 162 us (level)
  no operation moved by 1% of the time
where the time goes in v7:
time: 162 us
  blocking collectives  97.2 us (60%)
  waiting for transfers between devices  30.3 us (19%)
  starting transfers between devices  20.8 us (13%)
  Pallas kernels  5.79 us (4%)
  local copies, waits for them, and re-layouts  3.03 us (2%)
  other arithmetic  2.99 us (2%)
    all_to_all x6, blocking collectives, exchange(): return lax.all_to_all(parts, axes, 0, 0, tiled=True)  97.2 us
    all_to_all x2, waiting for transfers between devices, exchange(): return lax.all_to_all(parts, axes, 0, 0, tiled=True)  30.3 us
    all_to_all x2, starting transfers between devices, exchange(): return lax.all_to_all(parts, axes, 0, 0, tiled=True)  20.8 us
    pallas_call x3, Pallas kernels, tile_sum(): pl.pallas_call(functools.partial(tile_kernel, left is not None), out_shap...  3.56 us
  transfers between devices with their start and end apart: 2, of which 2 were waited for; matrix products, arithmetic and copies ran while one was open for 0% of the time, Pallas kernels for 0%

profile of v7, /device:TPU:1, one launch (start us, length us, event | category | flops | bytes accessed | tf_op | source)
XLA Modules:
  0.0 161.5 jit_solution(12306274597659368827)
XLA Ops:
  0.6 1.5 broadcast_in_dim.17
  2.1 17.2 %all-to-all-start = ((bf16[8,64,256]{2,1,0:T(8,128)(2,1)}), bf16[8,64,256]{2,1,0:T(8,128)(2,1)S(1)}, u32[]{:S(2)}, u32[]{:S(2)}) async-start(bf16[8,64,256]{2,1,0:T(8,128)(2,1)} %broadcast_in_dim.17), calls=%async_computation | async-start | bytes 524288 | tf_op jit(solution)/shard_map/all_to_all | solution.py:194
  20.0 0.7 fusion.13
  20.7 9.0 %all-to-all-done.pieces_ref = bf16[8,64,256]{2,1,0:T(8,128)(2,1)S(1)} async-done(((bf16[8,64,256]{2,1,0:T(8,128)(2,1)}), bf16[8,64,256]{2,1,0:T(8,128)(2,1)S(1)}, u32[]{:S(2)}, u32[]{:S(2)}) %all-to-all-start) | async-done | bytes 262176 | tf_op jit(solution)/shard_map/all_to_all | solution.py:194
  29.7 0.3 shard_map.60
  30.0 14.4 %all_to_all.40.grams_ref = bf16[8,72,128]{2,1,0:T(8,128)(2,1)S(1)} all-to-all(bf16[8,72,128]{2,1,0:T(8,128)(2,1)S(1)} %slice.68), channel_id=1, replica_groups=mesh['z'=8,'x'=8,'y'=8,'core'=2] {'x'}, dimensions={0} | all-to-all | bytes 294912 | tf_op jit(solution)/shard_map/all_to_all | solution.py:194
  44.4 1.8 %shard_map.61 = bf16[8,224,256]{2,1,0:T(8,128)(2,1)} custom-call(s32[8,128]{1,0:T(8,128)S(1)} %bitcast.13, bf16[8,64,256]{2,1,0:T(8,128)(2,1)S(1)} %all-to-all-done.pieces_ref, bf16[8,72,128]{2,1,0:T(8,128)(2,1)S(1)} %all_to_all.40.grams_ref), custom_call_target="tpu_custom_call" | custom-call | tf_op jit(solution)/shard_map/pallas_call | solution.py:91
  46.3 3.6 %all-to-all-start.2 = ((bf16[8,224,256]{2,1,0:T(8,128)(2,1)}), bf16[8,224,256]{2,1,0:T(8,128)(2,1)S(1)}, u32[]{:S(2)}, u32[]{:S(2)}) async-start(bf16[8,224,256]{2,1,0:T(8,128)(2,1)} %shard_map.61), calls=%async_computation.2 | async-start | bytes 1835008 | tf_op jit(solution)/shard_map/all_to_all | solution.py:194
  49.8 1.4 copy-done
  51.4 21.2 %all-to-all-done.2.factors_ref = bf16[8,224,256]{2,1,0:T(8,128)(2,1)S(1)} async-done(((bf16[8,224,256]{2,1,0:T(8,128)(2,1)}), bf16[8,224,256]{2,1,0:T(8,128)(2,1)S(1)}, u32[]{:S(2)}, u32[]{:S(2)}) %all-to-all-start.2) | async-done | bytes 917536 | tf_op jit(solution)/shard_map/all_to_all | solution.py:194
  72.6 0.8 shard_map.62
  73.4 23.8 %all_to_all.41 = s16[16,72,128]{2,1,0:T(8,128)(2,1)S(1)} all-to-all(s16[16,72,128]{2,1,0:T(8,128)(2,1)S(1)} %slice.70), channel_id=1, replica_groups=mesh['z'=8,'x'=8,'y'=8,'core'=2] {'y','core'}, dimensions={0} | all-to-all | bytes 589824 | tf_op jit(solution)/shard_map/all_to_all | solution.py:194
  97.2 0.2 fusion.9
  97.6 14.4 %all_to_all.42 = bf16[16,32,256]{2,1,0:T(8,128)(2,1)S(1)} all-to-all(bf16[16,32,256]{2,1,0:T(8,128)(2,1)S(1)} %broadcast_in_dim.18), channel_id=1, replica_groups=mesh['z'=8,'x'=8,'y'=8,'core'=2] {'y','core'}, dimensions={0} | all-to-all | bytes 524288 | tf_op jit(solution)/shard_map/all_to_all | solution.py:194
  112.0 1.4 shard_map.63
  113.5 15.1 %all_to_all.43 = s16[16,72,128]{2,1,0:T(8,128)(2,1)S(1)} all-to-all(s16[16,72,128]{2,1,0:T(8,128)(2,1)S(1)} %slice.75), channel_id=1, replica_groups=mesh['z'=8,'x'=8,'y'=8,'core'=2] {'y','core'}, dimensions={0} | all-to-all | bytes 589824 | tf_op jit(solution)/shard_map/all_to_all | solution.py:194
  128.5 0.2 fusion.10
  129.0 0.2 multiply_reduce_fusion.4
  129.3 14.4 %all_to_all.44 = bf16[16,32,256]{2,1,0:T(8,128)(2,1)S(1)} all-to-all(bf16[16,32,256]{2,1,0:T(8,128)(2,1)S(1)} %broadcast_in_dim.19), channel_id=1, replica_groups=mesh['z'=8,'x'=8,'y'=8,'core'=2] {'y','core'}, dimensions={0} | all-to-all | bytes 524288 | tf_op jit(solution)/shard_map/all_to_all | solution.py:194
  143.8 1.4 shard_map.64
  145.2 15.1 %all_to_all.45 = s16[16,72,128]{2,1,0:T(8,128)(2,1)S(1)} all-to-all(s16[16,72,128]{2,1,0:T(8,128)(2,1)S(1)} %slice.80), channel_id=1, replica_groups=mesh['z'=8,'x'=8,'y'=8,'core'=2] {'y','core'}, dimensions={0} | all-to-all | bytes 589824 | tf_op jit(solution)/shard_map/all_to_all | solution.py:194
  160.2 0.2 fusion.11
  160.6 0.2 multiply_reduce_fusion.3
  160.8 0.7 multiply_subtract_fusion
  (23 shorter events, 0.9 us)
Async XLA Ops:
  2.1 27.6 %all-to-all-start = ((bf16[8,64,256]{2,1,0:T(8,128)(2,1)}), bf16[8,64,256]{2,1,0:T(8,128)(2,1)S(1)}, u32[]{:S(2)}, u32[]{:S(2)}) async-start(bf16[8,64,256]{2,1,0:T(8,128)(2,1)} %broadcast_in_dim.17), calls=%async_computation | async-start | bytes 524288 | tf_op jit(solution)/shard_map/all_to_all | solution.py:194
  46.3 26.3 %all-to-all-start.2 = ((bf16[8,224,256]{2,1,0:T(8,128)(2,1)}), bf16[8,224,256]{2,1,0:T(8,128)(2,1)S(1)}, u32[]{:S(2)}, u32[]{:S(2)}) async-start(bf16[8,224,256]{2,1,0:T(8,128)(2,1)} %shard_map.61), calls=%async_computation.2 | async-start | bytes 1835008 | tf_op jit(solution)/shard_map/all_to_all | solution.py:194
  49.8 1.4 copy-start
